TPU v7x, 256 devices: a whole 4x4x8 slice. The times are simulated.
256 devices in a mesh: cp: 32 (over z, x), dp: 8 (over y, core).
Axes of the slice: x: 4, y: 4, z: 8, core: 2. Of those that a mesh axis runs over, the one named last changes fastest.
Arguments:
- llm_grads: bfloat16 [8, 1536, 8192], P('dp', 'cp'), may hold values from -6 to 6
- llm_owner: int32 [8, 1536], P('dp', 'cp'), may hold values from 0 to 1535, as said below
- image_ids: int32 [8, 1536], P('dp'), may hold values from 0 to 63, never falling along the last dimension, each value on 1 to 48 neighbouring positions
- stream: bfloat16 [8, 6144, 1280], P('dp', 'cp'), may hold values from -6 to 6
- ln_gain: float32 [1280], replicated, may hold values from 0.1 to 1.9
- pre_act: bfloat16 [8, 1536, 2560], P(None, 'cp', 'dp'), may hold values from -6 to 6
- w_in: bfloat16 [5120, 2560], P(None, 'dp'), may hold values from -0.078125 to 0.078125
- w_out: bfloat16 [2560, 8192], P('dp'), may hold values from -0.125 to 0.125
- qkv: bfloat16 [8, 6144, 3840], P('dp', 'cp'), may hold values from -5 to 5
- w_proj: bfloat16 [1280, 1280], P('cp'), may hold values from -0.15625 to 0.15625
Outputs:
- d_stream: bfloat16 [8, 6144, 1280], P('dp', 'cp')
- d_qkv: bfloat16 [8, 6144, 3840], P('dp', 'cp')
- d_proj: float32 [1280, 1280], P('cp')
- d_gain: float32 [1280], replicated
Inputs may be any that keep to these rules, and one draw needn't show every extreme that they name: Each row of llm_owner is a permutation of the 1536 merged tokens. The rows of one index of cp (aligned blocks of 48) send either exactly 3 or no rows to each block of 48 merged tokens.
All inputs are finite; a program needn't handle non-finite values.
Results may differ from a plain program's by a relative error of at most 0.033.
Values may be sent and summed in bfloat16 or wider, within the bound.
No kernel may reach another device: no remote copies, remote signals or barrier semaphores. Data moves between devices by JAX's collectives and lax.ppermute only.
A program may use at most 128 MiB of HBM per device.

v0:
```python
import math

import jax
import jax.numpy as jnp
from jax import lax
from jax.sharding import PartitionSpec as P

HEADS = 16
HEAD_DIM = 80


EPS = 1e-06


def extended(block, sides, width):
    for axis, dim in sides:
        count = lax.axis_size(axis)
        forward = [(i, i + 1) for i in range(count - 1)]
        backward = [(target, source) for source, target in forward]
        low = lax.ppermute(
            lax.slice_in_dim(block, block.shape[dim] - width, None, axis=dim), axis, forward
        )
        high = lax.ppermute(lax.slice_in_dim(block, 0, width, axis=dim), axis, backward)
        block = jnp.concatenate([low, block, high], axis=dim)
    return block


def from_behind(block, axis, distance):
    devices = range(lax.axis_size(axis))
    route = [(i - distance, i) for i in devices if i - distance in devices]
    return lax.ppermute(block, axis, route)


def gelu_slope(pre_value):
    normal_cdf = 0.5 * (1.0 + lax.erf(pre_value * 0.7071067811865476))
    density = jnp.exp(-0.5 * pre_value * pre_value) * 0.3989422804014327
    return normal_cdf + pre_value * density


def in_parts(vector):
    parts = []
    for _ in range(3):
        part = lax.reduce_precision(vector, 8, 7)
        parts.append(part.astype(jnp.bfloat16))
        vector = vector - part
    return jnp.stack(parts)


def block_forward(queries, key_heads, value_heads, seg_rows, seg_keys):
    single = jnp.float32
    narrow = jnp.bfloat16
    score_scale = 1.0 / math.sqrt(queries.shape[-1])
    scores = (
        jnp.einsum("qhe,khe->hqk", queries, key_heads, preferred_element_type=single) * score_scale
    )
    same_image = seg_rows[:, None] == seg_keys[None, :]
    scores = jnp.where(same_image[None], scores, -1e30)
    row_max = jnp.max(scores, axis=-1, keepdims=True)
    weights = jnp.exp(scores - row_max)
    probs = weights / jnp.sum(weights, axis=-1, keepdims=True)
    probs_low = probs.astype(narrow)
    attention = jnp.einsum(
        "hqk,khe->qhe", probs_low, value_heads, preferred_element_type=single
    ).astype(narrow)
    return (probs, probs_low, attention)


def block_backward(queries, key_heads, value_heads, d_heads, probs, probs_low, attention):
    single = jnp.float32
    narrow = jnp.bfloat16
    score_scale = 1.0 / math.sqrt(queries.shape[-1])
    d_probs = jnp.einsum("qhe,khe->hqk", d_heads, value_heads, preferred_element_type=single)
    row_delta = jnp.einsum("qhe,qhe->hq", d_heads, attention, preferred_element_type=single)
    d_scores = (probs * (d_probs - row_delta[:, :, None]) * score_scale).astype(narrow)
    d_query = jnp.einsum("hqk,khe->qhe", d_scores, key_heads, preferred_element_type=single)
    d_keys = jnp.einsum("hqk,qhe->khe", d_scores, queries, preferred_element_type=single)
    d_values = jnp.einsum("hqk,qhe->khe", probs_low, d_heads, preferred_element_type=single)
    return (d_query, d_keys, d_values)


def local(llm_grads, llm_owner, image_ids, stream, ln_gain, pre_act, w_in, w_out, qkv, w_proj):
    single = jnp.float32
    narrow = jnp.bfloat16
    shards = lax.axis_size("cp")
    batches = lax.axis_size("dp")
    device_index = lax.axis_index("cp")
    row_count = llm_grads.shape[1]
    patches = stream.shape[1]
    width = stream.shape[2]
    hidden = w_out.shape[0]
    slot_count = 2 * row_count // shards
    rows = batches * row_count
    packed_width = -(-(hidden + 1) // 128) * 128
    owners = lax.all_gather(llm_owner[0], "dp", axis=0)
    gathered = lax.all_gather(llm_grads[0], "dp", axis=0, tiled=True)
    share = w_proj.shape[0]
    part = share // batches
    own_proj = lax.dynamic_slice_in_dim(w_proj, lax.axis_index("dp") * part, part, 0)
    proj_parts = lax.all_to_all(
        jnp.broadcast_to(own_proj[None], (shards, part, width)),
        "cp",
        split_axis=0,
        concat_axis=0,
        tiled=True,
    ).reshape(shards * part, width)
    queries = qkv[0, :, :width].reshape(patches, HEADS, HEAD_DIM)
    key_values = extended(qkv[0, :, width:], (("cp", 0),), patches)
    gathered, key_values, proj_parts = lax.optimization_barrier(
        (gathered, key_values, proj_parts)
    )
    full_proj = lax.all_gather(proj_parts, "dp", axis=0, tiled=True)
    full_proj = full_proj.reshape(batches, shards, part, width)
    full_proj = full_proj.transpose(1, 0, 2, 3).reshape(width, width)
    target = owners // row_count
    place = (owners % row_count).reshape(rows, 1)
    same_target = target[:, :, None] == target[:, None, :]
    before = jnp.arange(row_count)[None, :] < jnp.arange(row_count)[:, None]
    rank = jnp.sum((same_target & before[None]).astype(jnp.int32), axis=2)
    batch_of = jnp.arange(batches, dtype=jnp.int32)[:, None]
    slot = ((target * batches + batch_of) * slot_count + rank).reshape(1, rows)
    slots = shards * batches * slot_count
    pick = (jnp.arange(slots, dtype=jnp.int32)[:, None] == slot).astype(narrow)
    d_rows = jnp.dot(gathered, w_out.T, preferred_element_type=single).astype(narrow)
    tags = jnp.where(
        jnp.arange(packed_width - hidden)[None, :] == 0, place + 1, 0
    ).astype(narrow)
    outgoing = jnp.dot(
        pick, jnp.concatenate([d_rows, tags], axis=1), preferred_element_type=single
    ).astype(narrow)
    arrived = lax.all_to_all(
        outgoing.reshape(shards, batches * slot_count, packed_width),
        "cp",
        split_axis=0,
        concat_axis=0,
        tiled=True,
    ).reshape(slots, packed_width)
    arrived, full_proj = lax.optimization_barrier((arrived, full_proj))
    tag_row = arrived[:, hidden].astype(jnp.int32).reshape(1, slots)
    slot_batch = (jnp.arange(slots, dtype=jnp.int32) // slot_count % batches)[None, :]
    home = jnp.where(tag_row > 0, slot_batch * row_count + tag_row - 1, -1)
    settle = (jnp.arange(rows, dtype=jnp.int32)[:, None] == home).astype(narrow)
    d_hidden = jnp.dot(settle, arrived, preferred_element_type=single)[:, :hidden].reshape(
        batches, row_count, hidden
    )
    saved_pre = pre_act.astype(single)
    d_pre = (d_hidden * gelu_slope(saved_pre)).astype(narrow)
    partials = jnp.einsum("bmh,ih->bmi", d_pre, w_in, preferred_element_type=single)
    d_norm = lax.psum_scatter(partials.astype(narrow), "dp", scatter_dimension=0, tiled=True)
    key_heads = key_values[:, :width].reshape(3 * patches, HEADS, HEAD_DIM)
    value_heads = key_values[:, width:].reshape(3 * patches, HEADS, HEAD_DIM)
    segment = jnp.repeat(image_ids[0], 4)
    seg_rim = jnp.full((patches,), -1, jnp.int32)
    seg_pad = jnp.concatenate([seg_rim, segment, seg_rim], axis=0)
    seg_keys = lax.dynamic_slice_in_dim(seg_pad, device_index * patches, 3 * patches, 0)
    seg_rows = lax.dynamic_slice_in_dim(segment, device_index * patches, patches, 0)
    probs, probs_low, attention = block_forward(
        queries, key_heads, value_heads, seg_rows, seg_keys
    )
    features = attention.reshape(patches, shards, batches, part)
    features = features.transpose(0, 2, 1, 3).reshape(patches, width)
    stream_wide = stream[0].astype(single)
    inverse = lax.rsqrt(jnp.mean(stream_wide * stream_wide, axis=-1, keepdims=True) + EPS)
    normed = stream_wide * inverse
    d_norm, features = lax.optimization_barrier((d_norm, features))
    d_norm = d_norm.astype(single).reshape(patches, width)
    gain_part = jnp.sum(d_norm * normed, axis=0)
    d_normed = d_norm * ln_gain
    d_stream = (
        inverse * (d_normed - normed * jnp.mean(d_normed * normed, axis=-1, keepdims=True))
    ).astype(narrow)
    d_proj_part = jnp.einsum(
        "pi,pj->ij", features, d_stream, preferred_element_type=single
    ).astype(narrow)
    d_proj_part, d_stream = lax.optimization_barrier((d_proj_part, d_stream))
    over_batches = lax.psum_scatter(d_proj_part, "dp", scatter_dimension=0, tiled=True)
    d_out = jnp.einsum(
        "pj,ij->pi", d_stream, full_proj, preferred_element_type=single
    ).astype(narrow)
    d_query, d_keys, d_values = block_backward(
        queries,
        key_heads,
        value_heads,
        d_out.reshape(patches, HEADS, HEAD_DIM),
        probs,
        probs_low,
        attention,
    )
    d_pairs = jnp.concatenate(
        [d_keys.reshape(3 * patches, width), d_values.reshape(3 * patches, width)], axis=1
    )
    from_prev = from_behind(d_pairs[2 * patches :].astype(jnp.bfloat16), "cp", 1).astype(
        jnp.float32
    )
    from_next = from_behind(d_pairs[:patches].astype(jnp.bfloat16), "cp", -1).astype(jnp.float32)
    own_part = d_pairs[patches : 2 * patches] + from_prev + from_next
    d_qkv = jnp.concatenate([d_query.reshape(patches, width), own_part], axis=1).astype(narrow)
    spread = jnp.concatenate(
        [
            over_batches.reshape(shards, part, width),
            jnp.broadcast_to(in_parts(gain_part)[None], (shards, 3, width)),
        ],
        axis=1,
    )
    per_shard = lax.all_to_all(spread, "cp", split_axis=0, concat_axis=0, tiled=True)
    totals = jnp.sum(per_shard.astype(single), axis=0)
    own_rows = jnp.concatenate(
        [totals[:part].astype(narrow), in_parts(jnp.sum(totals[part:], axis=0))], axis=0
    )
    whole = lax.all_gather(own_rows, "dp", axis=0).astype(single)
    d_proj = whole[:, :part].reshape(share, width)
    d_gain = jnp.sum(whole[:, part:], axis=(0, 1))
    return (d_stream[None], d_qkv[None], d_proj, d_gain)


def solution(mesh):
    in_specs = (
        P("dp", "cp", None),
        P("dp", "cp"),
        P("dp", None),
        P("dp", "cp", None),
        P(),
        P(None, "cp", "dp"),
        P(None, "dp"),
        P("dp", None),
        P("dp", "cp", None),
        P("cp", None),
    )
    out_specs = (P("dp", "cp", None), P("dp", "cp", None), P("cp", None), P())
    return jax.shard_map(local, mesh=mesh, in_specs=in_specs, out_specs=out_specs, check_vma=False)
```

profile of v0, /device:TPU:1, one launch (start us, length us, event | category | flops | bytes accessed | tf_op | source)
XLA Modules:
  0.0 279.5 jit_solution(6884850724870545361)
XLA Ops:
  8.0 2.4 slice_bitcast_fusion
  10.4 1.3 collective-permute-start.1
  11.7 5.5 %collective-permute-start = (bf16[192,2560]{1,0:T(8,128)(2,1)}, bf16[192,2560]{1,0:T(8,128)(2,1)}, u32[]{:S(2)}, u32[]{:S(2)}) collective-permute-start(bf16[192,2560]{1,0:T(8,128)(2,1)} %slice_bitcast_fusion), channel_id=1, source_target_pairs={{0,8},{8,16},{16,24},{24,32},{32,40},{40,48},{48,56},{56,64},{64,7... | collective-permute-start | bytes 2949128 | tf_op jit(solution)/shard_map/ppermute | solution.py:20
  18.0 44.9 %all_to_all.15 = bf16[32,5,1280]{2,1,0:T(8,128)(2,1)} all-to-all(bf16[32,5,1280]{2,1,0:T(8,128)(2,1)S(1)} %broadcast_in_dim.44), channel_id=1, replica_groups=mesh['cp'=32,'dp'=8] {'cp'}, dimensions={0} | all-to-all | bytes 819200 | tf_op jit(solution)/shard_map/all_to_all | solution.py:99
  63.0 2.0 reshape.315
  65.0 3.7 %pad_maximum_fusion.1 = bf16[576,2560]{1,0:T(8,128)(2,1)} fusion(bf16[192,2560]{1,0:T(8,128)(2,1)} %collective-permute-done.1, bf16[192,2560]{1,0:T(8,128)(2,1)} %slice_bitcast_fusion, bf16[192,2560]{1,0:T(8,128)(2,1)} %collective-permute-done), kind=kLoop, calls=%fused_computation.17 | loop fusion | flops 8847360 | bytes 5898240 | tf_op jit(solution)/shard_map/concatenate | solution.py:24
  68.7 16.2 %all-gather.2 = s32[8,1,48]{2,1,0:T(1,128)S(1)} all-gather(s32[1,1,48]{2,1,0:T(1,128)S(1)} %bitcast.130), channel_id=1, replica_groups=mesh['cp'=32,'dp'=8] {'dp'}, dimensions={0}, use_global_device_ids=true | all-gather | bytes 1728 | tf_op jit(solution)/shard_map/all_gather | solution.py:94
  85.5 7.3 %convolution_convert_fusion.6 = bf16[384,320]{0,1:T(8,128)(2,1)S(1)} fusion(bf16[384,8192]{1,0:T(8,128)(2,1)} %bitcast.131, bf16[320,8192]{1,0:T(8,128)(2,1)} %param.17), kind=kOutput, calls=%fused_computation.35 | convolution fusion | flops 2013388800 | bytes 11780096 | tf_op jit(solution)/shard_map/dot_general | solution.py:123
  92.9 1.3 convolution_convert_fusion.5
  94.2 4.6 %all-to-all-start.1 = ((bf16[32,24,384]{2,1,0:T(8,128)(2,1)}), bf16[32,24,384]{2,1,0:T(8,128)(2,1)}, u32[]{:S(2)}, u32[]{:S(2)}) async-start(bf16[32,24,384]{2,1,0:T(8,128)(2,1)} %bitcast.127), calls=%async_computation.1 | async-start | bytes 1179648 | tf_op jit(solution)/shard_map/all_to_all | solution.py:130
  98.9 1.5 all-gather.6.cloned.1.call-done
  100.4 7.0 %reshape.318 = bf16[8,32,5,1280]{3,2,1,0:T(8,128)(2,1)} reshape(bf16[1280,1280]{1,0:T(8,128)(2,1)} %all-gather.6.cloned.1.call-done) | data formatting | bytes 6553600 | tf_op jit(solution)/shard_map/reshape | solution.py:112
  107.4 5.5 %copy.69 = bf16[32,8,5,1280]{3,2,1,0:T(8,128)(2,1)} copy(bf16[32,8,5,1280]{3,2,0,1:T(8,128)(2,1)} %bitcast.110) | data formatting | bytes 6553600 | tf_op jit(solution)/shard_map/transpose | solution.py:113
  112.9 7.1 %reshape.319 = bf16[1280,1280]{1,0:T(8,128)(2,1)} reshape(bf16[32,8,5,1280]{3,2,1,0:T(8,128)(2,1)} %copy.69) | data formatting | bytes 6553600 | tf_op jit(solution)/shard_map/reshape | solution.py:113
  121.2 1.5 fusion.16
  122.8 5.2 %convolution_convert_fusion.1 = bf16[8,48,5120]{2,1,0:T(8,128)(2,1)} fusion(bf16[5120,320]{0,1:T(8,128)(2,1)S(1)} %copy-done, f32[8,48,320]{2,1,0:T(8,128)S(1)} %bitcast.132, bf16[8,48,320]{2,1,0:T(8,128)(2,1)} %param.15), kind=kOutput, calls=%fused_computation.8 | convolution fusion | flops 1261608960 | bytes 7946240 | tf_op jit(solution)/shard_map/bmh,ih->bmi/dot_general | solution.py:147
  128.3 2.0 slice.47
  131.4 1.6 reshape.322
  133.2 2.1 copy.73
  136.7 1.9 fusion.71
  138.6 2.0 copy.71
  140.6 2.4 copy.72
  143.1 7.9 %fusion.72 = (f32[16,192]{1,0:T(8,128)S(1)}, f32[16,192,576]{2,1,0:T(8,128)}) fusion(pred[192,576]{1,0:T(8,128)(4,1)S(1)} %broadcast_compare_fusion, bf16[576,16,80]{0,2,1:T(8,128)(2,1)S(1)} %bitcast.113, bf16[192,16,80]{0,2,1:T(8,128)(2,1)} %bitcast.124), kind=kOutput, calls=%fused_computation.134 | convolution fusion | flops 290193984 | bytes 9166848 | tf_op jit(solution)/shard_map/sub | solution.py:59
  150.9 3.8 %fusion.7 = bf16[16,192,576]{2,1,0:T(8,128)(2,1)S(1)} fusion(f32[16,192,576]{2,1,0:T(8,128)} %get-tuple-element.37, f32[16,192]{1,0:T(8,128)S(1)} %get-tuple-element.36), kind=kLoop, calls=%fused_computation.16 | loop fusion | flops 3538944 | bytes 10629120 | tf_op jit(solution)/shard_map/convert_element_type | solution.py:61
  154.8 1.9 copy-done.2
  156.7 1.6 convolution_convert_fusion.4
  159.6 1.3 copy.74
  161.4 3.4 %reduce-scatter.3.cloned.1.call-done = bf16[1,48,5120]{2,1,0:T(8,128)(2,1)} async-done(((bf16[8,48,5120]{2,1,0:T(8,128)(2,1)}), bf16[1,48,5120]{2,1,0:T(8,128)(2,1)}) %reduce-scatter.3.cloned.1.call-update) | async-done | bytes 491536 | tf_op jit(solution)/shard_map/reduce_scatter | solution.py:148
  164.8 1.3 reshape.336
  167.6 2.8 %convolution_convert_fusion = bf16[1280,1280]{1,0:T(8,128)(2,1)} fusion(bf16[192,1280]{0,1:T(8,128)(2,1)S(1)} %reshape.325, bf16[192,1280]{1,0:T(8,128)(2,1)S(1)} %fusion.20), kind=kOutput, calls=%fused_computation.4 | convolution fusion | flops 630784000 | bytes 4259840 | tf_op jit(solution)/shard_map/pi,pj->ij/dot_general | solution.py:171
  170.4 1.9 copy-done.5
  172.3 3.0 %convolution_convert_fusion.2 = bf16[192,1280]{1,0:T(8,128)(2,1)} fusion(bf16[192,1280]{1,0:T(8,128)(2,1)} %copy-done.13, bf16[1280,1280]{1,0:T(8,128)(2,1)S(1)} %copy-done.5), kind=kOutput, calls=%fused_computation.18 | convolution fusion | flops 629391360 | bytes 4259840 | tf_op jit(solution)/shard_map/pj,ij->pi/dot_general | solution.py:176
  176.6 5.0 %fusion.73 = f32[16,80,576]{2,1,0:T(8,128)} fusion(bf16[192,16,80]{0,2,1:T(8,128)(2,1)S(1)} %bitcast.118, bf16[16,192,576]{2,1,0:T(8,128)(2,1)} %copy-done.2), kind=kOutput, calls=%fused_computation.135 | convolution fusion | flops 283115520 | bytes 6979584 | tf_op jit(solution)/shard_map/hqk,qhe->khe/dot_general | solution.py:77
  181.6 2.6 copy.77
  184.2 2.5 fusion.12
  186.7 6.2 %multiply_convert_fusion = bf16[16,192,576]{2,1,0:T(8,128)(2,1)S(1)} fusion(f32[16,192]{1,0:T(8,128)S(1)} %fusion.12, f32[16,192,576]{2,1,0:T(8,128)} %get-tuple-element.37, f32[16,192]{1,0:T(8,128)S(1)} %get-tuple-element.36, bf16[192,16,80]{0,2,1:T(8,128)(2,1)} %bitcast.120, bf16[576,16,80]{0,2,1:T(8,128)(2,1)} %bitcast.116), kind=kOutput, calls=%fused_computation.2 | convolution fusion | flops 291962880 | bytes 12607488 | tf_op jit(solution)/shard_map/qhe,khe->hqk/dot_general | solution.py:72
  193.0 3.0 %fusion.74 = f32[16,576,80]{1,2,0:T(8,128)} fusion(bf16[192,16,80]{0,2,1:T(8,128)(2,1)S(1)} %bitcast.125, bf16[16,192,576]{2,1,0:T(8,128)(2,1)S(1)} %multiply_convert_fusion), kind=kOutput, calls=%fused_computation.136 | convolution fusion | flops 283115520 | bytes 6979584 | tf_op jit(solution)/shard_map/hqk,qhe->khe/dot_general | solution.py:76
  196.0 3.6 %copy.76 = f32[576,1280]{1,0:T(8,128)} copy(f32[576,1280]{0,1:T(8,128)} %bitcast.112) | data formatting | bytes 5898240 | tf_op jit(solution)/shard_map/reshape | solution.py:189
  199.6 2.2 fusion.2
  201.8 1.4 fusion.70
  203.2 1.3 collective-permute-start.3
  204.5 5.0 %collective-permute-start.2 = (bf16[192,2560]{1,0:T(8,128)(2,1)}, bf16[192,2560]{1,0:T(8,128)(2,1)}, u32[]{:S(2)}, u32[]{:S(2)}) collective-permute-start(bf16[192,2560]{1,0:T(8,128)(2,1)} %get-tuple-element.24), channel_id=1, source_target_pairs={{0,8},{8,16},{16,24},{24,32},{32,40},{40,48},{48,56},{56,64},{64,7... | collective-permute-start | bytes 2949128 | tf_op jit(solution)/shard_map/ppermute | solution.py:31
  211.9 10.3 %all-to-all-start.2 = ((bf16[32,8,1280]{2,1,0:T(8,128)(2,1)}), bf16[32,8,1280]{2,1,0:T(8,128)(2,1)}, u32[]{:S(2)}, u32[]{:S(2)}) async-start(bf16[32,8,1280]{2,1,0:T(8,128)(2,1)} %pad_maximum_fusion.3), calls=%async_computation.4 | async-start | bytes 1310720 | tf_op jit(solution)/shard_map/all_to_all | solution.py:204
  222.2 3.7 %convolution_convert_fusion.3 = bf16[16,80,192]{2,1,0:T(8,128)(2,1)S(1)} fusion(bf16[576,16,80]{0,2,1:T(8,128)(2,1)S(1)} %bitcast.114, bf16[16,192,576]{2,1,0:T(8,128)(2,1)} %copy-done.4), kind=kOutput, calls=%fused_computation.24 | convolution fusion | flops 283361280 | bytes 5505024 | tf_op jit(solution)/shard_map/hqk,khe->qhe/dot_general | solution.py:75
  227.0 2.5 fusion.23
  230.7 16.0 %all-to-all-done.2 = bf16[32,8,1280]{2,1,0:T(8,128)(2,1)} async-done(((bf16[32,8,1280]{2,1,0:T(8,128)(2,1)}), bf16[32,8,1280]{2,1,0:T(8,128)(2,1)}, u32[]{:S(2)}, u32[]{:S(2)}) %all-to-all-start.2) | async-done | bytes 655392 | tf_op jit(solution)/shard_map/all_to_all | solution.py:204
  248.0 21.8 %all-gather.1 = bf16[64,1280]{1,0:T(8,128)(2,1)S(1)} all-gather(bf16[8,1280]{1,0:T(8,128)(2,1)S(1)} %pad_maximum_fusion.4), channel_id=3, replica_groups=mesh['cp'=32,'dp'=8] {'dp'}, dimensions={0}, use_global_device_ids=true | all-gather | bytes 184320 | tf_op jit(solution)/shard_map/all_gather | solution.py:209
  271.2 1.7 reshape.332
  (94 shorter events, 18.3 us)
Async XLA Ops:
  7.2 115.6 %copy-start = (bf16[5120,320]{0,1:T(8,128)(2,1)S(1)}, bf16[5120,320]{0,1:T(8,128)(2,1)}, u32[]{:S(2)}) copy-start(bf16[5120,320]{0,1:T(8,128)(2,1)} %param.16) | copy-start | bytes 9830404
  7.2 61.5 %all-gather.8.cloned.1.call-start = ((), (), s32[]{:S(2)}) async-start(), calls=%async_computation.8 | async-start | bytes 7077888 | tf_op jit(solution)/shard_map/all_gather | solution.py:95
  7.9 92.5 %all-gather.6.cloned.1.call-start = ((), (), s32[]{:S(2)}) async-start(), calls=%async_computation.5 | async-start | bytes 3686400 | tf_op jit(solution)/shard_map/all_gather | solution.py:111
  10.4 54.6 %collective-permute-start.1 = (bf16[192,2560]{1,0:T(8,128)(2,1)}, bf16[192,2560]{1,0:T(8,128)(2,1)}, u32[]{:S(2)}, u32[]{:S(2)}) collective-permute-start(bf16[192,2560]{1,0:T(8,128)(2,1)} %slice_bitcast_fusion), channel_id=1, source_target_pairs={{8,0},{16,8},{24,16},{32,24},{40,32},{48,40},{56,48},{64,56},{72,6... | collective-permute-start | bytes 2949128 | tf_op jit(solution)/shard_map/ppermute | solution.py:23
  11.7 53.3 %collective-permute-start = (bf16[192,2560]{1,0:T(8,128)(2,1)}, bf16[192,2560]{1,0:T(8,128)(2,1)}, u32[]{:S(2)}, u32[]{:S(2)}) collective-permute-start(bf16[192,2560]{1,0:T(8,128)(2,1)} %slice_bitcast_fusion), channel_id=1, source_target_pairs={{0,8},{8,16},{16,24},{24,32},{32,40},{40,48},{48,56},{56,64},{64,7... | collective-permute-start | bytes 2949128 | tf_op jit(solution)/shard_map/ppermute | solution.py:20
  65.0 3.7 %copy-start.19 = (s32[1,48]{1,0:T(1,128)S(1)}, s32[1,48]{1,0:T(1,128)}, u32[]{:S(2)}) copy-start(s32[1,48]{1,0:T(1,128)} %param.11) | copy-start | bytes 580
  94.2 25.8 %all-to-all-start.1 = ((bf16[32,24,384]{2,1,0:T(8,128)(2,1)}), bf16[32,24,384]{2,1,0:T(8,128)(2,1)}, u32[]{:S(2)}, u32[]{:S(2)}) async-start(bf16[32,24,384]{2,1,0:T(8,128)(2,1)} %bitcast.127), calls=%async_computation.1 | async-start | bytes 1179648 | tf_op jit(solution)/shard_map/all_to_all | solution.py:130
  98.9 66.0 %reduce-scatter.3.cloned.1.call-start = ((), (), s32[]{:S(2)}) async-start(), calls=%async_computation.6 | async-start | bytes 4423680 | tf_op jit(solution)/shard_map/reduce_scatter | solution.py:148
  128.0 2.3 copy-start.18
  128.0 8.7 %copy-start.6 = (bf16[576,2560]{1,0:T(8,128)(2,1)S(1)}, bf16[576,2560]{1,0:T(8,128)(2,1)}, u32[]{:S(2)}) copy-start(bf16[576,2560]{1,0:T(8,128)(2,1)} %pad_maximum_fusion.1) | copy-start | bytes 8847364
  128.0 81.5 %reduce-scatter.5.cloned.1.call-start = ((), (), s32[]{:S(2)}) async-start(), calls=%async_computation.7 | async-start | bytes 3686400 | tf_op jit(solution)/shard_map/reduce_scatter | solution.py:175
  140.6 14.2 %copy-start.9 = (bf16[576,1280]{0,1:T(8,128)(2,1)}, bf16[576,1280]{0,1:T(8,128)(2,1)S(1)}, u32[]{:S(2)}) copy-start(bf16[576,1280]{0,1:T(8,128)(2,1)S(1)} %copy.71) | copy-start | bytes 4423684
  143.1 7.9 %copy-start.7 = (bf16[576,1280]{0,1:T(8,128)(2,1)}, bf16[576,1280]{0,1:T(8,128)(2,1)S(1)}, u32[]{:S(2)}) copy-start(bf16[576,1280]{0,1:T(8,128)(2,1)S(1)} %copy.72) | copy-start | bytes 4423684
  154.8 1.9 copy-start.2
  158.3 3.1 %copy-start.10 = (bf16[16,80,192]{2,1,0:T(8,128)(2,1)}, bf16[16,80,192]{2,1,0:T(8,128)(2,1)S(1)}, u32[]{:S(2)}) copy-start(bf16[16,80,192]{2,1,0:T(8,128)(2,1)S(1)} %convolution_convert_fusion.4) | copy-start | bytes 1474564
  158.3 7.8 %copy-start.12 = (bf16[1,192,1280]{2,1,0:T(8,128)(2,1)S(1)}, bf16[1,192,1280]{2,1,0:T(8,128)(2,1)}, u32[]{:S(2)}) copy-start(bf16[1,192,1280]{2,1,0:T(8,128)(2,1)} %param.13) | copy-start | bytes 1474564
  158.4 7.8 %copy-start.17 = (f32[1280]{0:T(1024)S(1)}, f32[1280]{0:T(1024)}, u32[]{:S(2)}) copy-start(f32[1280]{0:T(1024)} %param.14) | copy-start | bytes 15364
  166.8 0.8 copy-start.13
  170.4 1.9 copy-start.5
  176.6 5.0 %copy-start.11 = (bf16[192,1280]{0,1:T(8,128)(2,1)}, bf16[192,1280]{0,1:T(8,128)(2,1)S(1)}, u32[]{:S(2)}) copy-start(bf16[192,1280]{0,1:T(8,128)(2,1)S(1)} %copy.75) | copy-start | bytes 1474564
  184.2 15.4 %copy-start.3 = (f32[576,1280]{1,0:T(8,128)}, f32[576,1280]{1,0:T(8,128)S(1)}, u32[]{:S(2)}) copy-start(f32[576,1280]{1,0:T(8,128)S(1)} %copy.77) | copy-start | bytes 8847364
  186.7 6.2 %copy-start.14 = (bf16[1,192,1280]{1,2,0:T(8,128)(2,1)S(1)}, bf16[1,192,1280]{1,2,0:T(8,128)(2,1)}, u32[]{:S(2)}) copy-start(bf16[1,192,1280]{1,2,0:T(8,128)(2,1)} %copy.73) | copy-start | bytes 1474564
  192.9 3.0 %copy-start.4 = (bf16[16,192,576]{2,1,0:T(8,128)(2,1)}, bf16[16,192,576]{2,1,0:T(8,128)(2,1)S(1)}, u32[]{:S(2)}) copy-start(bf16[16,192,576]{2,1,0:T(8,128)(2,1)S(1)} %multiply_convert_fusion) | copy-start | bytes 10616836
  201.8 20.5 %copy-start.8 = (bf16[576,1280]{0,1:T(8,128)(2,1)S(1)}, bf16[576,1280]{0,1:T(8,128)(2,1)}, u32[]{:S(2)}) copy-start(bf16[576,1280]{0,1:T(8,128)(2,1)} %copy-done.7) | copy-start | bytes 4423684
  203.2 23.8 %collective-permute-start.3 = (bf16[192,2560]{1,0:T(8,128)(2,1)}, bf16[192,2560]{1,0:T(8,128)(2,1)}, u32[]{:S(2)}, u32[]{:S(2)}) collective-permute-start(bf16[192,2560]{1,0:T(8,128)(2,1)} %get-tuple-element.25), channel_id=1, source_target_pairs={{8,0},{16,8},{24,16},{32,24},{40,32},{48,40},{56,48},{64,56},{72,6... | collective-permute-start | bytes 2949128 | tf_op jit(solution)/shard_map/ppermute | solution.py:31
  204.5 22.5 %collective-permute-start.2 = (bf16[192,2560]{1,0:T(8,128)(2,1)}, bf16[192,2560]{1,0:T(8,128)(2,1)}, u32[]{:S(2)}, u32[]{:S(2)}) collective-permute-start(bf16[192,2560]{1,0:T(8,128)(2,1)} %get-tuple-element.24), channel_id=1, source_target_pairs={{0,8},{8,16},{16,24},{24,32},{32,40},{40,48},{48,56},{56,64},{64,7... | collective-permute-start | bytes 2949128 | tf_op jit(solution)/shard_map/ppermute | solution.py:31
  211.9 34.8 %all-to-all-start.2 = ((bf16[32,8,1280]{2,1,0:T(8,128)(2,1)}), bf16[32,8,1280]{2,1,0:T(8,128)(2,1)}, u32[]{:S(2)}, u32[]{:S(2)}) async-start(bf16[32,8,1280]{2,1,0:T(8,128)(2,1)} %pad_maximum_fusion.3), calls=%async_computation.4 | async-start | bytes 1310720 | tf_op jit(solution)/shard_map/all_to_all | solution.py:204
  227.0 2.6 copy-start.16
  227.0 46.0 %copy-start.1 = (bf16[5120,320]{0,1:T(8,128)(2,1)S(1)}, bf16[5120,320]{0,1:T(8,128)(2,1)}, u32[]{:S(2)}) copy-start(bf16[5120,320]{0,1:T(8,128)(2,1)} %param.16) | copy-start | bytes 9830404
  269.9 0.7 copy-start.15
Sparse Core Ops, SparseCore 0:
  9.8 47.6 all-gather.7
  68.8 31.6 all-gather.5
  128.2 36.6 reduce-scatter.2
  170.5 37.4 reduce-scatter.4
where the time goes:
time: 281 us; the launch traced here: 279 us
  blocking collectives  83 us (30%)
  local copies, waits for them, and re-layouts  60.9 us (22%)
  matrix products  48.7 us (17%)
  starting transfers between devices  28.3 us (10%)
  other arithmetic  22.7 us (8%)
  waiting for transfers between devices  21.7 us (8%)
  between operations  14.2 us (5%)
    all_to_all x1, blocking collectives, local(): lax.all_to_all(jnp.broadcast_to(own_proj[None], (shards, part, width)), '...  44.9 us
    all_gather x1, blocking collectives, local(): whole = lax.all_gather(own_rows, 'dp', axis=0).astype(single)  21.8 us
    all_gather x1, blocking collectives, local(): owners = lax.all_gather(llm_owner[0], 'dp', axis=0)  16.2 us
    all_to_all x1, waiting for transfers between devices, local(): lax.all_to_all(spread, 'cp', split_axis=0, concat_axis=0, tiled=True)  16 us
    all_to_all x1, starting transfers between devices, local(): lax.all_to_all(spread, 'cp', split_axis=0, concat_axis=0, tiled=True)  10.3 us
    sub x1, matrix products, block_forward(): weights = jnp.exp(scores - row_max)  7.88 us
    dot_general x1, matrix products, local(): jnp.dot(gathered, w_out.T, preferred_element_type=single).astype(narrow)  7.34 us
    reshape x1, local copies, waits for them, and re-layouts, local(): full_proj = full_proj.transpose(1, 0, 2, 3).reshape(width, width)  7.14 us
  transfers between devices with their start and end apart: 10, of which 3 were waited for; matrix products, arithmetic and copies ran while one was open for 40% of the time, Pallas kernels for 0%

commit v1 on v0

v1 whole, which is shorter than its diff:
```python
import math

import jax
import jax.numpy as jnp
from jax import lax
from jax.experimental import pallas as pl
from jax.experimental.pallas import tpu as pltpu
from jax.sharding import PartitionSpec as P

HEADS = 16
HEAD_DIM = 80


EPS = 1e-06


def from_behind(block, axis, distance):
    devices = range(lax.axis_size(axis))
    route = [(i - distance, i) for i in devices if i - distance in devices]
    return lax.ppermute(block, axis, route)


def by_core(block, dim, own):
    core = lax.axis_index("dp") % 2
    return lax.dynamic_index_in_dim(block, core if own else 1 - core, dim, keepdims=False)


def added_on_chip(partial_of):
    count = lax.axis_size("dp")
    swap = [(i, i ^ 1) for i in range(count)]
    received = lax.ppermute(partial_of(False).astype(jnp.bfloat16), "dp", swap)
    return (partial_of(True) + received.astype(jnp.float32)).astype(jnp.bfloat16)


def scattered_over_y(pair):
    count = lax.axis_size("dp")
    groups = [list(range(core, count, 2)) for core in range(2)]
    return lax.psum_scatter(
        pair, "dp", scatter_dimension=0, axis_index_groups=groups, tiled=True
    )


def gelu_slope(pre_value):
    normal_cdf = 0.5 * (1.0 + lax.erf(pre_value * 0.7071067811865476))
    density = jnp.exp(-0.5 * pre_value * pre_value) * 0.3989422804014327
    return normal_cdf + pre_value * density


def in_parts(vector):
    parts = []
    for _ in range(3):
        part = lax.reduce_precision(vector, 8, 7)
        parts.append(part.astype(jnp.bfloat16))
        vector = vector - part
    return jnp.stack(parts)


GROUP = 8
CONTRACT_LAST = (((1,), (1,)), ((), ()))
CONTRACT_FIRST = (((0,), (0,)), ((), ()))
CONTRACT_INNER = (((1,), (0,)), ((), ()))


def mxu(a, b, dims):
    return lax.dot_general(a, b, dims, preferred_element_type=jnp.float32)


def head_columns(ref, head):
    return ref[..., head * HEAD_DIM : (head + 1) * HEAD_DIM]


def window(low_ref, own_ref, high_ref, head):
    parts = [head_columns(low_ref, head), head_columns(own_ref, head)[0]]
    return jnp.concatenate(parts + [head_columns(high_ref, head)], axis=0)


def forward_kernel(q_ref, k_ref, v_ref, kl_ref, vl_ref, kh_ref, vh_ref, rows_ref, keys_ref,
                   att_ref, lse_ref):
    scale = 1.0 / math.sqrt(HEAD_DIM)
    mask = rows_ref[...] == keys_ref[...]
    outs = []
    stats = []
    for head in range(GROUP):
        queries = head_columns(q_ref, head)[0]
        key_heads = window(kl_ref, k_ref, kh_ref, head)
        value_heads = window(vl_ref, v_ref, vh_ref, head)
        scores = jnp.where(mask, mxu(queries, key_heads, CONTRACT_LAST) * scale, -1e30)
        row_max = jnp.max(scores, axis=-1, keepdims=True)
        weights = jnp.exp(scores - row_max)
        total = jnp.sum(weights, axis=-1, keepdims=True)
        probs_low = (weights * (1.0 / total)).astype(jnp.bfloat16)
        outs.append(mxu(probs_low, value_heads, CONTRACT_INNER).astype(jnp.bfloat16))
        stats.append(row_max + jnp.log(total))
    att_ref[...] = jnp.concatenate(outs, axis=1)
    lse_ref[0] = jnp.concatenate(stats, axis=1)


def backward_kernel(q_ref, k_ref, v_ref, kl_ref, vl_ref, kh_ref, vh_ref, rows_ref, keys_ref,
                    att_ref, lse_ref, do_ref,
                    dq_ref, low_ref, own_ref, high_ref):
    scale = 1.0 / math.sqrt(HEAD_DIM)
    narrow = jnp.bfloat16
    patches = dq_ref.shape[0]
    mask = rows_ref[...] == keys_ref[...]
    d_query = []
    d_pairs = ([], [])
    for head in range(GROUP):
        queries = head_columns(q_ref, head)[0]
        key_heads = window(kl_ref, k_ref, kh_ref, head)
        value_heads = window(vl_ref, v_ref, vh_ref, head)
        d_heads = head_columns(do_ref, head)
        scores = jnp.where(mask, mxu(queries, key_heads, CONTRACT_LAST) * scale, -1e30)
        probs = jnp.exp(scores - lse_ref[0, :, head : head + 1])
        probs_low = probs.astype(narrow)
        delta = jnp.sum(
            d_heads.astype(jnp.float32) * head_columns(att_ref, head).astype(jnp.float32),
            axis=-1,
            keepdims=True,
        )
        d_probs = mxu(d_heads, value_heads, CONTRACT_LAST)
        d_scores = (probs * ((d_probs - delta) * scale)).astype(narrow)
        d_query.append(mxu(d_scores, key_heads, CONTRACT_INNER).astype(narrow))
        d_pairs[0].append(mxu(d_scores, queries, CONTRACT_FIRST))
        d_pairs[1].append(mxu(probs_low, d_heads, CONTRACT_FIRST))
    dq_ref[...] = jnp.concatenate(d_query, axis=1)
    for i in range(2):
        total = jnp.concatenate(d_pairs[i], axis=1)
        low_ref[i] = total[:patches].astype(narrow)
        own_ref[i] = total[patches : 2 * patches]
        high_ref[i] = total[2 * patches :].astype(narrow)


def attention_calls(qkv, low, high, seg_rows, seg_keys):
    patches = qkv.shape[1]
    width = qkv.shape[2] // 3
    lanes = GROUP * HEAD_DIM
    groups = width // lanes
    own = [
        pl.BlockSpec((1, patches, lanes), lambda g, i=i: (0, 0, i * groups + g)) for i in range(3)
    ]
    halo = [
        pl.BlockSpec((patches, lanes), lambda g, i=i: (0, i * groups + g)) for i in (0, 1, 0, 1)
    ]
    ids = [
        pl.BlockSpec((patches, 1), lambda g: (0, 0)),
        pl.BlockSpec((1, 3 * patches), lambda g: (0, 0)),
    ]
    operands = (qkv, qkv, qkv, low, low, high, high, seg_rows[:, None], seg_keys[None, :])
    flat = pl.BlockSpec((patches, lanes), lambda g: (0, g))
    stat = pl.BlockSpec((1, patches, GROUP), lambda g: (g, 0, 0))
    pair = pl.BlockSpec((2, patches, lanes), lambda g: (0, 0, g))
    params = pltpu.CompilerParams(vmem_limit_bytes=48 * 1024 * 1024)
    flops = 2 * 3 * patches * patches * width
    exps = 3 * patches * patches * HEADS

    def cost(dots):
        return pl.CostEstimate(
            flops=dots * flops, bytes_accessed=12 * patches * width, transcendentals=exps
        )

    attention, stats = pl.pallas_call(
        forward_kernel,
        grid=(groups,),
        in_specs=own + halo + ids,
        out_specs=(flat, stat),
        out_shape=(
            jax.ShapeDtypeStruct((patches, width), jnp.bfloat16),
            jax.ShapeDtypeStruct((groups, patches, GROUP), jnp.float32),
        ),
        compiler_params=params,
        cost_estimate=cost(2),
        name="attention_forward",
    )(*operands)

    def backward(d_out):
        return pl.pallas_call(
            backward_kernel,
            grid=(groups,),
            in_specs=own + halo + ids + [flat, stat, flat],
            out_specs=(flat, pair, pair, pair),
            out_shape=(
                jax.ShapeDtypeStruct((patches, width), jnp.bfloat16),
                jax.ShapeDtypeStruct((2, patches, width), jnp.bfloat16),
                jax.ShapeDtypeStruct((2, patches, width), jnp.float32),
                jax.ShapeDtypeStruct((2, patches, width), jnp.bfloat16),
            ),
            compiler_params=params,
            cost_estimate=cost(5),
            name="attention_backward",
        )(*operands, attention, stats, d_out)

    return attention, backward


def local(llm_grads, llm_owner, image_ids, stream, ln_gain, pre_act, w_in, w_out, qkv, w_proj):
    single = jnp.float32
    narrow = jnp.bfloat16
    shards = lax.axis_size("cp")
    batches = lax.axis_size("dp")
    device_index = lax.axis_index("cp")
    row_count = llm_grads.shape[1]
    patches = stream.shape[1]
    width = stream.shape[2]
    hidden = w_out.shape[0]
    slot_count = 2 * row_count // shards
    rows = batches * row_count
    packed_width = -(-(hidden + 1) // 128) * 128
    owners = lax.all_gather(llm_owner[0], "dp", axis=0)
    gathered = lax.all_gather(llm_grads[0], "dp", axis=0, tiled=True)
    share = w_proj.shape[0]
    part = share // batches
    own_proj = lax.dynamic_slice_in_dim(w_proj, lax.axis_index("dp") * part, part, 0)
    own_proj, owners = lax.optimization_barrier((own_proj, owners))
    proj_parts = lax.all_to_all(
        jnp.broadcast_to(own_proj[None], (shards, part, width)),
        "cp",
        split_axis=0,
        concat_axis=0,
        tiled=True,
    ).reshape(shards * part, width)
    gathered, proj_parts = lax.optimization_barrier((gathered, proj_parts))
    full_proj = lax.all_gather(proj_parts, "dp", axis=0, tiled=True)
    low = from_behind(qkv[0, :, width:], "cp", 1)
    high = from_behind(qkv[0, :, width:], "cp", -1)
    target = owners // row_count
    place = (owners % row_count).reshape(rows, 1)
    same_target = target[:, :, None] == target[:, None, :]
    before = jnp.arange(row_count)[None, :] < jnp.arange(row_count)[:, None]
    rank = jnp.sum((same_target & before[None]).astype(jnp.int32), axis=2)
    batch_of = jnp.arange(batches, dtype=jnp.int32)[:, None]
    slot = ((target * batches + batch_of) * slot_count + rank).reshape(1, rows)
    slots = shards * batches * slot_count
    pick = (jnp.arange(slots, dtype=jnp.int32)[:, None] == slot).astype(narrow)
    d_rows = jnp.dot(gathered, w_out.T, preferred_element_type=single).astype(narrow)
    tags = jnp.where(
        jnp.arange(packed_width - hidden)[None, :] == 0, place + 1, 0
    ).astype(narrow)
    outgoing = jnp.dot(
        pick, jnp.concatenate([d_rows, tags], axis=1), preferred_element_type=single
    ).astype(narrow)
    arrived = lax.all_to_all(
        outgoing.reshape(shards, batches * slot_count, packed_width),
        "cp",
        split_axis=0,
        concat_axis=0,
        tiled=True,
    ).reshape(slots, packed_width)
    arrived, full_proj = lax.optimization_barrier((arrived, full_proj))
    tag_row = arrived[:, hidden].astype(jnp.int32).reshape(1, slots)
    slot_batch = (jnp.arange(slots, dtype=jnp.int32) // slot_count % batches)[None, :]
    home = jnp.where(tag_row > 0, slot_batch * row_count + tag_row - 1, -1)
    settle = (jnp.arange(rows, dtype=jnp.int32)[:, None] == home).astype(narrow)
    d_hidden = jnp.dot(settle, arrived, preferred_element_type=single)[:, :hidden].reshape(
        batches, row_count, hidden
    )
    saved_pre = pre_act.astype(single)
    d_pre = (d_hidden * gelu_slope(saved_pre)).astype(narrow)
    d_norm = added_on_chip(
        lambda own: (
            jnp.einsum(
                "bmh,ih->bmi",
                by_core(d_pre.reshape(batches // 2, 2, row_count, hidden), 1, own),
                w_in,
                preferred_element_type=single,
            )
        )
    )
    d_norm = scattered_over_y(d_norm)
    segment = jnp.repeat(image_ids[0], 4)
    seg_rim = jnp.full((patches,), -1, jnp.int32)
    seg_pad = jnp.concatenate([seg_rim, segment, seg_rim], axis=0)
    seg_keys = lax.dynamic_slice_in_dim(seg_pad, device_index * patches, 3 * patches, 0)
    seg_rows = lax.dynamic_slice_in_dim(segment, device_index * patches, patches, 0)
    attention, backward = attention_calls(qkv, low, high, seg_rows, seg_keys)
    features = attention.reshape(patches, shards, batches // 2, 2, part)
    features = features.transpose(0, 3, 2, 1, 4).reshape(patches, 2, width // 2)
    stream_wide = stream[0].astype(single)
    inverse = lax.rsqrt(jnp.mean(stream_wide * stream_wide, axis=-1, keepdims=True) + EPS)
    normed = stream_wide * inverse
    d_norm, features = lax.optimization_barrier((d_norm, features))
    d_norm = lax.optimization_barrier(d_norm.reshape(patches, width)).astype(single)
    gain_part = jnp.sum(d_norm * normed, axis=0)
    d_normed = d_norm * ln_gain
    d_stream = (
        inverse * (d_normed - normed * jnp.mean(d_normed * normed, axis=-1, keepdims=True))
    ).astype(narrow)
    d_stream = lax.optimization_barrier(d_stream)
    d_proj_pair = added_on_chip(
        lambda own: jnp.einsum(
            "pi,pj->ij", by_core(features, 1, own), d_stream, preferred_element_type=single
        )
    )
    d_out = jnp.einsum(
        "pj,ij->pi", d_stream, full_proj, preferred_element_type=single
    ).astype(narrow)
    row = jnp.arange(width, dtype=jnp.int32)
    natural = row // part % shards * share + row // (part * shards) * part + row % part
    order = (natural[:, None] == jnp.arange(width, dtype=jnp.int32)[None, :]).astype(narrow)
    d_out = jnp.dot(d_out, order, preferred_element_type=single).astype(narrow)
    d_proj_pair, d_out = lax.optimization_barrier((d_proj_pair, d_out))
    over_batches = scattered_over_y(d_proj_pair)
    d_query, d_low, d_own, d_high = backward(d_out)
    from_prev = from_behind(d_high, "cp", 1)
    from_next = from_behind(d_low, "cp", -1)
    spread = jnp.concatenate(
        [
            over_batches.reshape(shards, part, width),
            jnp.broadcast_to(in_parts(gain_part)[None], (shards, 3, width)),
        ],
        axis=1,
    )
    per_shard = lax.all_to_all(spread, "cp", split_axis=0, concat_axis=0, tiled=True)
    per_shard, from_prev, from_next = lax.optimization_barrier((per_shard, from_prev, from_next))
    d_pairs = (d_own + from_prev.astype(single) + from_next.astype(single)).astype(narrow)
    d_qkv = jnp.concatenate([d_query, d_pairs[0], d_pairs[1]], axis=1)
    totals = jnp.sum(per_shard.astype(single), axis=0)
    own_rows = jnp.concatenate(
        [totals[:part].astype(narrow), in_parts(jnp.sum(totals[part:], axis=0))], axis=0
    )
    whole = lax.all_gather(own_rows, "dp", axis=0).astype(single)
    d_proj = whole[:, :part].reshape(share, width)
    d_gain = jnp.sum(whole[:, part:], axis=(0, 1))
    return (d_stream[None], d_qkv[None], d_proj, d_gain)


def solution(mesh):
    in_specs = (
        P("dp", "cp", None),
        P("dp", "cp"),
        P("dp", None),
        P("dp", "cp", None),
        P(),
        P(None, "cp", "dp"),
        P(None, "dp"),
        P("dp", None),
        P("dp", "cp", None),
        P("cp", None),
    )
    out_specs = (P("dp", "cp", None), P("dp", "cp", None), P("cp", None), P())
    return jax.shard_map(local, mesh=mesh, in_specs=in_specs, out_specs=out_specs, check_vma=False)
```

time: 281 us -> 312 us (1.11)
  waiting for transfers between devices: 21.7 us -> 92.7 us
  Pallas kernels: 0 us -> 30.5 us
  blocking collectives: 83 us -> 57.6 us
  local copies, waits for them, and re-layouts: 60.9 us -> 38.9 us
  matrix products: 48.7 us -> 27.2 us
  other arithmetic: 22.7 us -> 15.1 us
  starting transfers between devices: 28.3 us -> 32.7 us
    ppermute x2 -> x4, waiting for transfers between devices: 0.01 us -> 40.2 us  [from_behind(): return lax.ppermute(block, axis, route)]
    pallas_call x0 -> x2, Pallas kernels: none -> 30.5 us  [the longest x1 17.8 us: backward(): pl.pallas_call(backward_kernel, grid=(groups,), in_specs=own + halo + ids...]
    reduce_scatter x2, waiting for transfers between devices: 3.43 us -> 25.6 us  [scattered_over_y(): lax.psum_scatter(pair, 'dp', scatter_dimension=0, axis_index_groups=group...]
    reshape x7 -> x2, local copies, waits for them, and re-layouts: 23.4 us -> 4.33 us  [the longest x1 2.22 us: local(): features = attention.reshape(patches, shards, batches // 2, 2, part)]
    all_to_all x1, waiting for transfers between devices: 0.01 us -> 17.7 us  [local(): lax.all_to_all(outgoing.reshape(shards, batches * slot_count, packed_widt...]
    all_to_all x1, waiting for transfers between devices: 16 us -> 0.01 us  [local(): lax.all_to_all(spread, 'cp', split_axis=0, concat_axis=0, tiled=True)]
    all_to_all x1, blocking collectives: 44.9 us -> 29.9 us  [local(): lax.all_to_all(jnp.broadcast_to(own_proj[None], (shards, part, width)), '...]
    dot_general x8 -> x5, matrix products: 30.6 us -> 17.1 us  [the longest x2 6.64 us: local(): jnp.einsum('bmh,ih->bmi', by_core(d_pre.reshape(batches // 2, 2, row_coun...]
  transfers between devices with their start and end apart: 10 -> 12, of which waited for: 3 -> 8; matrix products, arithmetic and copies ran while one was open for 40% -> 11% of each run, Pallas kernels for 0% -> 10%
where the time goes in v1:
time: 312 us; the launch traced here: 309 us
  waiting for transfers between devices  92.7 us (30%)
  blocking collectives  57.6 us (18%)
  local copies, waits for them, and re-layouts  38.9 us (12%)
  starting transfers between devices  32.7 us (10%)
  Pallas kernels  30.5 us (10%)
  matrix products  27.2 us (9%)
  other arithmetic  15.1 us (5%)
  between operations  14.1 us (5%)
    ppermute x4, waiting for transfers between devices, from_behind(): return lax.ppermute(block, axis, route)  40.2 us
    all_to_all x1, blocking collectives, local(): lax.all_to_all(jnp.broadcast_to(own_proj[None], (shards, part, width)), '...  29.9 us
    reduce_scatter x2, waiting for transfers between devices, scattered_over_y(): lax.psum_scatter(pair, 'dp', scatter_dimension=0, axis_index_groups=group...  25.6 us
    pallas_call x1, Pallas kernels, backward(): pl.pallas_call(backward_kernel, grid=(groups,), in_specs=own + halo + ids...  17.8 us
    all_to_all x1, waiting for transfers between devices, local(): lax.all_to_all(outgoing.reshape(shards, batches * slot_count, packed_widt...  17.7 us
    all_gather x1, blocking collectives, local(): whole = lax.all_gather(own_rows, 'dp', axis=0).astype(single)  15.3 us
    pallas_call x1, Pallas kernels, attention_calls(): pl.pallas_call(forward_kernel, grid=(groups,), in_specs=own + halo + ids,...  12.7 us
    all_gather x1, blocking collectives, local(): owners = lax.all_gather(llm_owner[0], 'dp', axis=0)  12.4 us
  transfers between devices with their start and end apart: 12, of which 8 were waited for; matrix products, arithmetic and copies ran while one was open for 11% of the time, Pallas kernels for 10%

profile of v1, /device:TPU:1, one launch (start us, length us, event | category | flops | bytes accessed | tf_op | source)
XLA Modules:
  0.0 308.8 jit_solution(17173745574017585744)
XLA Ops:
  8.0 12.4 %all-gather.2 = s32[8,1,48]{2,1,0:T(1,128)S(1)} all-gather(s32[1,1,48]{2,1,0:T(1,128)} %bitcast.73), channel_id=1, replica_groups=mesh['cp'=32,'dp'=8] {'dp'}, dimensions={0}, use_global_device_ids=true | all-gather | bytes 1728 | tf_op jit(solution)/shard_map/all_gather | solution.py:208
  21.2 29.9 %all_to_all.15 = bf16[32,5,1280]{2,1,0:T(8,128)(2,1)} all-to-all(bf16[32,5,1280]{2,1,0:T(8,128)(2,1)S(1)} %broadcast_in_dim.38), channel_id=1, replica_groups=mesh['cp'=32,'dp'=8] {'cp'}, dimensions={0} | all-to-all | bytes 819200 | tf_op jit(solution)/shard_map/all_to_all | solution.py:214
  51.1 2.0 reshape.244
  53.1 4.5 %all-gather.8.cloned.1.call-done = bf16[1,384,8192]{2,1,0:T(8,128)(2,1)} async-done(((bf16[1,48,8192]{2,1,0:T(8,128)(2,1)}), bf16[1,384,8192]{2,1,0:T(8,128)(2,1)}) %all-gather.8.cloned.1.call-update) | async-done | bytes 6291472 | tf_op jit(solution)/shard_map/all_gather | solution.py:209
  58.2 7.2 %convolution_convert_fusion.4 = bf16[384,320]{0,1:T(8,128)(2,1)S(1)} fusion(bf16[384,8192]{1,0:T(8,128)(2,1)} %bitcast.74, bf16[320,8192]{1,0:T(8,128)(2,1)} %param.17), kind=kOutput, calls=%fused_computation.22 | convolution fusion | flops 2013388800 | bytes 11780096 | tf_op jit(solution)/shard_map/dot_general | solution.py:234
  65.4 1.3 convolution_convert_fusion.3
  66.8 9.6 %all-to-all-start.1 = ((bf16[32,24,384]{2,1,0:T(8,128)(2,1)}), bf16[32,24,384]{2,1,0:T(8,128)(2,1)}, u32[]{:S(2)}, u32[]{:S(2)}) async-start(bf16[32,24,384]{2,1,0:T(8,128)(2,1)} %bitcast.68), calls=%async_computation.1 | async-start | bytes 1179648 | tf_op jit(solution)/shard_map/all_to_all | solution.py:241
  76.5 17.7 %all-to-all-done.1 = bf16[32,24,384]{2,1,0:T(8,128)(2,1)} async-done(((bf16[32,24,384]{2,1,0:T(8,128)(2,1)}), bf16[32,24,384]{2,1,0:T(8,128)(2,1)}, u32[]{:S(2)}, u32[]{:S(2)}) %all-to-all-start.1) | async-done | bytes 589856 | tf_op jit(solution)/shard_map/all_to_all | solution.py:241
  95.4 1.5 fusion.11
  97.0 1.2 fusion.28
  98.2 2.5 convolution_convert_fusion
  100.8 2.1 collective-permute-start
  102.9 3.9 %collective-permute-done = bf16[4,48,5120]{2,1,0:T(8,128)(2,1)} collective-permute-done((bf16[4,48,5120]{2,1,0:T(8,128)(2,1)}, bf16[4,48,5120]{2,1,0:T(8,128)(2,1)}, u32[]{:S(2)}, u32[]{:S(2)}) %collective-permute-start) | collective-permute-done | bytes 1966112 | tf_op jit(solution)/shard_map/ppermute | solution.py:31
  106.8 4.1 %add_convert_fusion = bf16[4,48,5120]{2,1,0:T(8,128)(2,1)} fusion(bf16[4,48,5120]{2,1,0:T(8,128)(2,1)} %collective-permute-done, bf16[5120,320]{0,1:T(8,128)(2,1)S(1)} %copy-done, bf16[4,2,48,320]{3,2,1,0:T(8,128)(2,1)} %bitcast.67, s32[]{:T(128)S(6)} %select_n.117), kind=kOutput, calls=%fused_computation.3 | convolution fusion | flops 632094720 | bytes 7356420 | tf_op jit(solution)/shard_map/bmh,ih->bmi/dot_general | solution.py:260
  111.0 2.2 slice_bitcast_fusion
  113.2 3.7 %collective-permute-start.1 = (bf16[192,2560]{1,0:T(8,128)(2,1)}, bf16[192,2560]{1,0:T(8,128)(2,1)}, u32[]{:S(2)}, u32[]{:S(2)}) collective-permute-start(bf16[192,2560]{1,0:T(8,128)(2,1)} %slice_bitcast_fusion), channel_id=1, source_target_pairs={{0,8},{8,16},{16,24},{24,32},{32,40},{40,48},{48,56},{56,64},{64,7... | collective-permute-start | bytes 2949128 | tf_op jit(solution)/shard_map/ppermute | solution.py:20
  116.9 1.5 collective-permute-start.2
  119.6 1.6 reshape.249
  121.6 1.2 fusion.17
  122.8 14.2 %collective-permute-done.1.kl_ref.vl_ref = bf16[192,2560]{1,0:T(8,128)(2,1)} collective-permute-done((bf16[192,2560]{1,0:T(8,128)(2,1)}, bf16[192,2560]{1,0:T(8,128)(2,1)}, u32[]{:S(2)}, u32[]{:S(2)}) %collective-permute-start.1) | collective-permute-done | bytes 983072 | tf_op jit(solution)/shard_map/ppermute | solution.py:20
  137.0 4.8 %collective-permute-done.2.kh_ref.vh_ref = bf16[192,2560]{1,0:T(8,128)(2,1)} collective-permute-done((bf16[192,2560]{1,0:T(8,128)(2,1)}, bf16[192,2560]{1,0:T(8,128)(2,1)}, u32[]{:S(2)}, u32[]{:S(2)}) %collective-permute-start.2) | collective-permute-done | bytes 983072 | tf_op jit(solution)/shard_map/ppermute | solution.py:20
  141.8 1.4 copy-done.1
  143.1 12.7 %attention_forward.1 = (bf16[192,1280]{1,0:T(8,128)(2,1)S(1)}, f32[2,192,8]{2,1,0:T(8,128)S(1)}) custom-call(bf16[1,192,3840]{2,1,0:T(8,128)(2,1)S(1)} %copy-done.1, bf16[1,192,3840]{2,1,0:T(8,128)(2,1)S(1)} %copy-done.1, bf16[1,192,3840]{2,1,0:T(8,128)(2,1)S(1)} %copy-done.1, bf16[192,2560]{1,0:T(8,128)(2,1)} %collective-permute-done.1.kl_ref.vl_ref, ...), custom_call_target="tpu_custom_call" | custom-call | flops 566231040 | bytes 2949120 | tf_op jit(solution)/shard_map/attention_forward/pallas_call | solution.py:161
  157.3 2.1 copy.49
  159.4 2.2 reshape.250
  161.6 2.6 copy.50
  164.3 3.7 %constant_dynamic-slice_fusion.1 = (bf16[192,1,640]{0,1,2:T(2,128)(2,1)}, bf16[192,1,640]{0,1,2:T(2,128)(2,1)}) fusion(bf16[192,2,640]{0,1,2:T(2,128)(2,1)} %bitcast.62, s32[]{:T(128)S(6)} %select_n.117, s32[]{:T(128)S(6)} %select_n.118), kind=kLoop, calls=%fused_computation.130 | loop fusion | bytes 983048 | tf_op jit(solution)/shard_map/jit(dynamic_index_in_dim)/dynamic_slice | solution.py:25
  168.0 1.9 copy.52
  170.0 2.1 reshape.252
  172.1 1.7 fusion.16
  173.7 1.5 fusion.14
  176.0 1.8 convolution_convert_fusion.1
  177.8 1.5 collective-permute-start.3
  179.3 2.0 copy.51
  181.3 5.1 %fusion.7.do_ref = bf16[192,1280]{1,0:T(8,128)(2,1)} fusion(s32[1280]{0:T(1024)S(1)} %fusion.49, bf16[192,1280]{1,0:T(8,128)(2,1)} %copy-done.9, bf16[1280,1280]{1,0:T(8,128)(2,1)} %all-gather.6.cloned.1.call-done), kind=kOutput, calls=%fused_computation.11 | convolution fusion | flops 1260421120 | bytes 4264960 | tf_op jit(solution)/shard_map/dot_general | solution.py:299
  186.4 3.5 %add_convert_fusion.1 = bf16[640,1280]{1,0:T(8,128)(2,1)} fusion(bf16[640,1280]{1,0:T(8,128)(2,1)} %collective-permute-done.3, bf16[192,1280]{1,0:T(8,128)(2,1)} %copy-done.9, bf16[192,1,640]{2,0,1:T(8,128)(2,1)} %copy.51), kind=kOutput, calls=%fused_computation.8 | convolution fusion | flops 317030400 | bytes 4014080 | tf_op jit(solution)/shard_map/pi,pj->ij/dot_general | solution.py:289
  190.0 25.6 %reduce-scatter.5.cloned.1.call-done = bf16[160,1280]{1,0:T(8,128)(2,1)} async-done(((bf16[640,1280]{1,0:T(8,128)(2,1)}), bf16[160,1280]{1,0:T(8,128)(2,1)}) %reduce-scatter.5.cloned.1.call-update) | async-done | bytes 409616 | tf_op jit(solution)/shard_map/reduce_scatter | solution.py:38
  215.6 2.0 reshape.253
  217.7 2.3 pad_maximum_fusion
  220.0 9.7 %all-to-all-start.2 = ((bf16[32,8,1280]{2,1,0:T(8,128)(2,1)}), bf16[32,8,1280]{2,1,0:T(8,128)(2,1)}, u32[]{:S(2)}, u32[]{:S(2)}) async-start(bf16[32,8,1280]{2,1,0:T(8,128)(2,1)} %pad_maximum_fusion), calls=%async_computation.4 | async-start | bytes 1310720 | tf_op jit(solution)/shard_map/all_to_all | solution.py:312
  232.7 17.8 %attention_backward.1 = (bf16[192,1280]{1,0:T(8,128)(2,1)S(1)}, bf16[2,192,1280]{2,1,0:T(8,128)(2,1)S(1)}, f32[2,192,1280]{2,1,0:T(8,128)}, bf16[2,192,1280]{2,1,0:T(8,128)(2,1)S(1)}) custom-call(bf16[1,192,3840]{2,1,0:T(8,128)(2,1)} %v_ref.3, bf16[1,192,3840]{2,1,0:T(8,128)(2,1)} %v_ref.3, bf16[1,192,3840]{2,1,0:T(8,128)(2,1)} %v_ref.3, ...), custom_call_target="tpu_custom_call" | custom-call | flops 1415577600 | bytes 2949120 | tf_op jit(solution)/shard_map/attention_backward/pallas_call | solution.py:176
  251.3 3.1 %collective-permute-start.4 = (bf16[2,192,1280]{2,1,0:T(8,128)(2,1)S(1)}, bf16[2,192,1280]{2,1,0:T(8,128)(2,1)S(1)}, u32[]{:S(2)}, u32[]{:S(2)}) collective-permute-start(bf16[2,192,1280]{2,1,0:T(8,128)(2,1)S(1)} %get-tuple-element.37), channel_id=1, source_target_pairs={{0,8},{8,16},{16,24},{24,32},{32,40},{40,48},{48,56},{56,64},{64,7... | collective-permute-start | bytes 2949128 | tf_op jit(solution)/shard_map/ppermute | solution.py:20
  254.5 1.3 collective-permute-start.5
  255.8 18.2 %collective-permute-done.4 = bf16[2,192,1280]{2,1,0:T(8,128)(2,1)S(1)} collective-permute-done((bf16[2,192,1280]{2,1,0:T(8,128)(2,1)S(1)}, bf16[2,192,1280]{2,1,0:T(8,128)(2,1)S(1)}, u32[]{:S(2)}, u32[]{:S(2)}) %collective-permute-start.4) | collective-permute-done | bytes 983072 | tf_op jit(solution)/shard_map/ppermute | solution.py:20
  274.9 3.1 collective-permute-done.5
  279.2 15.3 %all-gather.1 = bf16[64,1280]{1,0:T(8,128)(2,1)S(1)} all-gather(bf16[8,1280]{1,0:T(8,128)(2,1)S(1)} %pad_maximum_fusion.1), channel_id=3, replica_groups=mesh['cp'=32,'dp'=8] {'dp'}, dimensions={0}, use_global_device_ids=true | all-gather | bytes 184320 | tf_op jit(solution)/shard_map/all_gather | solution.py:320
  295.9 1.7 reshape.254
  297.6 2.4 add_convert_fusion.2
  (78 shorter events, 17.1 us)
Async XLA Ops:
  7.2 91.1 %copy-start = (bf16[5120,320]{0,1:T(8,128)(2,1)S(1)}, bf16[5120,320]{0,1:T(8,128)(2,1)}, u32[]{:S(2)}) copy-start(bf16[5120,320]{0,1:T(8,128)(2,1)} %param.16) | copy-start | bytes 9830404
  7.2 50.4 %all-gather.8.cloned.1.call-start = ((), (), s32[]{:S(2)}) async-start(), calls=%async_computation.8 | async-start | bytes 7077888 | tf_op jit(solution)/shard_map/all_gather | solution.py:209
  7.9 86.3 %all-gather.6.cloned.1.call-start = ((), (), s32[]{:S(2)}) async-start(), calls=%async_computation.5 | async-start | bytes 3686400 | tf_op jit(solution)/shard_map/all_gather | solution.py:222
  66.8 27.4 %all-to-all-start.1 = ((bf16[32,24,384]{2,1,0:T(8,128)(2,1)}), bf16[32,24,384]{2,1,0:T(8,128)(2,1)}, u32[]{:S(2)}, u32[]{:S(2)}) async-start(bf16[32,24,384]{2,1,0:T(8,128)(2,1)} %bitcast.68), calls=%async_computation.1 | async-start | bytes 1179648 | tf_op jit(solution)/shard_map/all_to_all | solution.py:241
  76.4 87.9 %reduce-scatter.3.cloned.1.call-start = ((), (), s32[]{:S(2)}) async-start(), calls=%async_computation.6 | async-start | bytes 2457600 | tf_op jit(solution)/shard_map/reduce_scatter | solution.py:38
  98.2 2.5 copy-start.13
  100.8 6.0 %collective-permute-start = (bf16[4,48,5120]{2,1,0:T(8,128)(2,1)}, bf16[4,48,5120]{2,1,0:T(8,128)(2,1)}, u32[]{:S(2)}, u32[]{:S(2)}) collective-permute-start(bf16[4,48,5120]{2,1,0:T(8,128)(2,1)} %convolution_convert_fusion), channel_id=1, source_target_pairs={{0,1},{1,0},{2,3},{3,2},{4,5},{5,4},{6,7},{7,6},{8,9},{9,8},{10,11... | collective-permute-start | bytes 5898248 | tf_op jit(solution)/shard_map/ppermute | solution.py:31
  110.9 7.5 %copy-start.15 = (s32[1,1536]{1,0:T(1,128)S(1)}, s32[1,1536]{1,0:T(1,128)}, u32[]{:S(2)}) copy-start(s32[1,1536]{1,0:T(1,128)} %param.12) | copy-start | bytes 18436
  111.0 104.7 %reduce-scatter.5.cloned.1.call-start = ((), (), s32[]{:S(2)}) async-start(), calls=%async_computation.7 | async-start | bytes 2048000 | tf_op jit(solution)/shard_map/reduce_scatter | solution.py:38
  113.2 23.8 %collective-permute-start.1 = (bf16[192,2560]{1,0:T(8,128)(2,1)}, bf16[192,2560]{1,0:T(8,128)(2,1)}, u32[]{:S(2)}, u32[]{:S(2)}) collective-permute-start(bf16[192,2560]{1,0:T(8,128)(2,1)} %slice_bitcast_fusion), channel_id=1, source_target_pairs={{0,8},{8,16},{16,24},{24,32},{32,40},{40,48},{48,56},{56,64},{64,7... | collective-permute-start | bytes 2949128 | tf_op jit(solution)/shard_map/ppermute | solution.py:20
  116.9 24.8 %collective-permute-start.2 = (bf16[192,2560]{1,0:T(8,128)(2,1)}, bf16[192,2560]{1,0:T(8,128)(2,1)}, u32[]{:S(2)}, u32[]{:S(2)}) collective-permute-start(bf16[192,2560]{1,0:T(8,128)(2,1)} %slice_bitcast_fusion), channel_id=1, source_target_pairs={{8,0},{16,8},{24,16},{32,24},{40,32},{48,40},{56,48},{64,56},{72,6... | collective-permute-start | bytes 2949128 | tf_op jit(solution)/shard_map/ppermute | solution.py:20
  141.8 1.4 copy-start.1
  155.8 0.8 copy-start.2
  156.6 0.7 copy-start.7
  164.3 7.8 %copy-start.14 = (f32[1280]{0:T(1024)S(1)}, f32[1280]{0:T(1024)}, u32[]{:S(2)}) copy-start(f32[1280]{0:T(1024)} %param.14) | copy-start | bytes 15364
  172.1 3.9 %copy-start.12 = (bf16[192,1,640]{2,0,1:T(8,128)(2,1)S(1)}, bf16[192,1,640]{2,0,1:T(8,128)(2,1)}, u32[]{:S(2)}) copy-start(bf16[192,1,640]{2,0,1:T(8,128)(2,1)} %copy.52) | copy-start | bytes 737284
  175.2 0.8 copy-start.9
  177.8 8.6 %collective-permute-start.3 = (bf16[640,1280]{1,0:T(8,128)(2,1)}, bf16[640,1280]{1,0:T(8,128)(2,1)}, u32[]{:S(2)}, u32[]{:S(2)}) collective-permute-start(bf16[640,1280]{1,0:T(8,128)(2,1)} %convolution_convert_fusion.1), channel_id=1, source_target_pairs={{0,1},{1,0},{2,3},{3,2},{4,5},{5,4},{6,7},{7,6},{8,9},{9,8},{10,11... | collective-permute-start | bytes 4915208 | tf_op jit(solution)/shard_map/ppermute | solution.py:31
  220.0 58.0 %all-to-all-start.2 = ((bf16[32,8,1280]{2,1,0:T(8,128)(2,1)}), bf16[32,8,1280]{2,1,0:T(8,128)(2,1)}, u32[]{:S(2)}, u32[]{:S(2)}) async-start(bf16[32,8,1280]{2,1,0:T(8,128)(2,1)} %pad_maximum_fusion), calls=%async_computation.4 | async-start | bytes 1310720 | tf_op jit(solution)/shard_map/all_to_all | solution.py:312
  229.7 1.0 copy-start.3
  230.7 1.0 copy-start.6
  231.8 0.9 copy-start.8
  250.6 0.8 copy-start.4
  251.3 22.6 %collective-permute-start.4 = (bf16[2,192,1280]{2,1,0:T(8,128)(2,1)S(1)}, bf16[2,192,1280]{2,1,0:T(8,128)(2,1)S(1)}, u32[]{:S(2)}, u32[]{:S(2)}) collective-permute-start(bf16[2,192,1280]{2,1,0:T(8,128)(2,1)S(1)} %get-tuple-element.37), channel_id=1, source_target_pairs={{0,8},{8,16},{16,24},{24,32},{32,40},{40,48},{48,56},{56,64},{64,7... | collective-permute-start | bytes 2949128 | tf_op jit(solution)/shard_map/ppermute | solution.py:20
  254.5 23.5 %collective-permute-start.5 = (bf16[2,192,1280]{2,1,0:T(8,128)(2,1)S(1)}, bf16[2,192,1280]{2,1,0:T(8,128)(2,1)}, u32[]{:S(2)}, u32[]{:S(2)}) collective-permute-start(bf16[2,192,1280]{2,1,0:T(8,128)(2,1)S(1)} %get-tuple-element.38), channel_id=1, source_target_pairs={{8,0},{16,8},{24,16},{32,24},{40,32},{48,40},{56,48},{64,56},{72,6... | collective-permute-start | bytes 2949128 | tf_op jit(solution)/shard_map/ppermute | solution.py:20
  273.9 0.9 copy-start.11
  294.6 0.7 copy-start.10
  300.0 1.0 copy-start.5
Sparse Core Ops, SparseCore 0:
  9.8 47.6 all-gather.7
  60.0 30.9 all-gather.5
  111.1 26.0 reduce-scatter.2
  190.1 25.5 reduce-scatter.4

commit v2 on v1

--- a/solution.py
+++ b/solution.py
@@ -205,12 +205,10 @@
     slot_count = 2 * row_count // shards
     rows = batches * row_count
     packed_width = -(-(hidden + 1) // 128) * 128
-    owners = lax.all_gather(llm_owner[0], "dp", axis=0)
     gathered = lax.all_gather(llm_grads[0], "dp", axis=0, tiled=True)
     share = w_proj.shape[0]
     part = share // batches
     own_proj = lax.dynamic_slice_in_dim(w_proj, lax.axis_index("dp") * part, part, 0)
-    own_proj, owners = lax.optimization_barrier((own_proj, owners))
     proj_parts = lax.all_to_all(
         jnp.broadcast_to(own_proj[None], (shards, part, width)),
         "cp",
@@ -218,10 +216,14 @@
         concat_axis=0,
         tiled=True,
     ).reshape(shards * part, width)
-    gathered, proj_parts = lax.optimization_barrier((gathered, proj_parts))
+    proj_parts, key_values, own_owners = lax.optimization_barrier(
+        (proj_parts, qkv[0, :, width:], llm_owner[0])
+    )
+    owners = lax.all_gather(own_owners, "dp", axis=0)
+    gathered, proj_parts, owners = lax.optimization_barrier((gathered, proj_parts, owners))
     full_proj = lax.all_gather(proj_parts, "dp", axis=0, tiled=True)
-    low = from_behind(qkv[0, :, width:], "cp", 1)
-    high = from_behind(qkv[0, :, width:], "cp", -1)
+    low = from_behind(key_values, "cp", 1)
+    high = from_behind(key_values, "cp", -1)
     target = owners // row_count
     place = (owners % row_count).reshape(rows, 1)
     same_target = target[:, :, None] == target[:, None, :]
@@ -232,6 +234,7 @@
     slots = shards * batches * slot_count
     pick = (jnp.arange(slots, dtype=jnp.int32)[:, None] == slot).astype(narrow)
     d_rows = jnp.dot(gathered, w_out.T, preferred_element_type=single).astype(narrow)
+    d_rows, low, high = lax.optimization_barrier((d_rows, low, high))
     tags = jnp.where(
         jnp.arange(packed_width - hidden)[None, :] == 0, place + 1, 0
     ).astype(narrow)
@@ -272,12 +275,23 @@
     seg_keys = lax.dynamic_slice_in_dim(seg_pad, device_index * patches, 3 * patches, 0)
     seg_rows = lax.dynamic_slice_in_dim(segment, device_index * patches, patches, 0)
     attention, backward = attention_calls(qkv, low, high, seg_rows, seg_keys)
-    features = attention.reshape(patches, shards, batches // 2, 2, part)
-    features = features.transpose(0, 3, 2, 1, 4).reshape(patches, 2, width // 2)
+    column = jnp.arange(width // 2, dtype=jnp.int32)
+    column_base = column // part % shards * share + column // (part * shards) * (2 * part)
+    column_base = (column_base + column % part)[None, :]
+    feature = jnp.arange(width, dtype=jnp.int32)[:, None]
+    core = lax.axis_index("dp") % 2
+
+    def features_of(core):
+        pick_columns = (feature == column_base + core * part).astype(narrow)
+        return jnp.dot(attention, pick_columns, preferred_element_type=single).astype(narrow)
+
+    other_features, own_features = features_of(1 - core), features_of(core)
     stream_wide = stream[0].astype(single)
     inverse = lax.rsqrt(jnp.mean(stream_wide * stream_wide, axis=-1, keepdims=True) + EPS)
     normed = stream_wide * inverse
-    d_norm, features = lax.optimization_barrier((d_norm, features))
+    d_norm, other_features, own_features = lax.optimization_barrier(
+        (d_norm, other_features, own_features)
+    )
     d_norm = lax.optimization_barrier(d_norm.reshape(patches, width)).astype(single)
     gain_part = jnp.sum(d_norm * normed, axis=0)
     d_normed = d_norm * ln_gain
@@ -287,7 +301,10 @@
     d_stream = lax.optimization_barrier(d_stream)
     d_proj_pair = added_on_chip(
         lambda own: jnp.einsum(
-            "pi,pj->ij", by_core(features, 1, own), d_stream, preferred_element_type=single
+            "pi,pj->ij",
+            own_features if own else other_features,
+            d_stream,
+            preferred_element_type=single,
         )
     )
     d_out = jnp.einsum(
@@ -300,6 +317,7 @@
     d_proj_pair, d_out = lax.optimization_barrier((d_proj_pair, d_out))
     over_batches = scattered_over_y(d_proj_pair)
     d_query, d_low, d_own, d_high = backward(d_out)
+    over_batches, d_query = lax.optimization_barrier((over_batches, d_query))
     from_prev = from_behind(d_high, "cp", 1)
     from_next = from_behind(d_low, "cp", -1)
     spread = jnp.concatenate(

time: 312 us -> 286 us (0.917)
  blocking collectives: 57.6 us -> 24.3 us
  starting transfers between devices: 32.7 us -> 47.5 us
  local copies, waits for them, and re-layouts: 38.9 us -> 26.1 us
  matrix products: 27.2 us -> 31.1 us
    all_to_all x1 -> x0, blocking collectives: 29.9 us -> none  [local(): lax.all_to_all(jnp.broadcast_to(own_proj[None], (shards, part, width)), '...]
    reduce_scatter x2, waiting for transfers between devices: 25.6 us -> 7.75 us  [scattered_over_y(): lax.psum_scatter(pair, 'dp', scatter_dimension=0, axis_index_groups=group...]
    all_to_all x0 -> x1, waiting for transfers between devices: none -> 14.5 us  [local(): lax.all_to_all(jnp.broadcast_to(own_proj[None], (shards, part, width)), '...]
    all_gather x1 -> x0, blocking collectives: 12.4 us -> none  [local(): owners = lax.all_gather(llm_owner[0], 'dp', axis=0)]
    all_to_all x0 -> x1, starting transfers between devices: none -> 12 us  [local(): lax.all_to_all(jnp.broadcast_to(own_proj[None], (shards, part, width)), '...]
    unnamed x0 -> x1, blocking collectives: none -> 10.3 us
    dynamic_slice x3 -> x0, local copies, waits for them, and re-layouts: 7.61 us -> none  [by_core(): lax.dynamic_index_in_dim(block, core if own else 1 - core, dim, keepdims=...]
    dot_general x2 -> x4, matrix products: 5.3 us -> 9.29 us  [the longest x2 6.26 us: local(): jnp.einsum('pi,pj->ij', own_features if own else other_features, d_stream...]
  transfers between devices with their start and end apart: 12 -> 13, of which waited for: 8 -> 10; matrix products, arithmetic and copies ran while one was open for 11% -> 10% of each run, Pallas kernels for 10% -> 11%
where the time goes in v2:
time: 286 us; the launch traced here: 281 us
  waiting for transfers between devices  91.7 us (32%)
  starting transfers between devices  47.5 us (17%)
  matrix products  31.1 us (11%)
  Pallas kernels  30.6 us (11%)
  local copies, waits for them, and re-layouts  26.1 us (9%)
  blocking collectives  24.3 us (8%)
  other arithmetic  15.1 us (5%)
  between operations  14.8 us (5%)
    ppermute x4, waiting for transfers between devices, from_behind(): return lax.ppermute(block, axis, route)  43.7 us
    pallas_call x1, Pallas kernels, backward(): pl.pallas_call(backward_kernel, grid=(groups,), in_specs=own + halo + ids...  17.9 us
    all_to_all x1, waiting for transfers between devices, local(): lax.all_to_all(outgoing.reshape(shards, batches * slot_count, packed_widt...  16.4 us
    all_to_all x1, waiting for transfers between devices, local(): lax.all_to_all(jnp.broadcast_to(own_proj[None], (shards, part, width)), '...  14.5 us
    all_gather x1, blocking collectives, local(): whole = lax.all_gather(own_rows, 'dp', axis=0).astype(single)  14 us
    pallas_call x1, Pallas kernels, attention_calls(): pl.pallas_call(forward_kernel, grid=(groups,), in_specs=own + halo + ids,...  12.8 us
    all_to_all x1, starting transfers between devices, local(): lax.all_to_all(jnp.broadcast_to(own_proj[None], (shards, part, width)), '...  12 us
    all_to_all x1, starting transfers between devices, local(): lax.all_to_all(outgoing.reshape(shards, batches * slot_count, packed_widt...  10.8 us
  transfers between devices with their start and end apart: 13, of which 10 were waited for; matrix products, arithmetic and copies ran while one was open for 10% of the time, Pallas kernels for 11%

profile of v2, /device:TPU:1, one launch (start us, length us, event | category | flops | bytes accessed | tf_op | source)
XLA Modules:
  0.0 281.2 jit_solution(3623863579983276614)
XLA Ops:
  9.8 12.0 %all-to-all-start = ((bf16[32,5,1280]{2,1,0:T(8,128)(2,1)}), bf16[32,5,1280]{2,1,0:T(8,128)(2,1)}, u32[]{:S(2)}, u32[]{:S(2)}) async-start(bf16[32,5,1280]{2,1,0:T(8,128)(2,1)} %broadcast_in_dim.38), calls=%async_computation | async-start | bytes 1310720 | tf_op jit(solution)/shard_map/all_to_all | solution.py:212
  21.8 1.3 dynamic-slice
  23.7 2.2 slice_bitcast_fusion
  25.9 14.5 %all-to-all-done = bf16[32,5,1280]{2,1,0:T(8,128)(2,1)} async-done(((bf16[32,5,1280]{2,1,0:T(8,128)(2,1)}), bf16[32,5,1280]{2,1,0:T(8,128)(2,1)}, u32[]{:S(2)}, u32[]{:S(2)}) %all-to-all-start) | async-done | bytes 409632 | tf_op jit(solution)/shard_map/all_to_all | solution.py:212
  40.4 2.0 reshape.284
  42.6 10.3 %all-reduce = s32[384]{0:T(512)S(1)} all-reduce(s32[384]{0:T(512)S(1)} %dynamic-update-slice), channel_id=3, replica_groups=mesh['cp'=32,'dp'=8] {'dp'}, use_global_device_ids=true, to_apply=%add | all-reduce | flops 384 | bytes 3072
  53.0 4.7 %all-gather.8.cloned.1.call-done = bf16[1,384,8192]{2,1,0:T(8,128)(2,1)} async-done(((bf16[1,48,8192]{2,1,0:T(8,128)(2,1)}), bf16[1,384,8192]{2,1,0:T(8,128)(2,1)}) %all-gather.8.cloned.1.call-update) | async-done | bytes 6291472 | tf_op jit(solution)/shard_map/all_gather | solution.py:208
  57.7 4.1 %collective-permute-start = (bf16[192,2560]{1,0:T(8,128)(2,1)}, bf16[192,2560]{1,0:T(8,128)(2,1)}, u32[]{:S(2)}, u32[]{:S(2)}) collective-permute-start(bf16[192,2560]{1,0:T(8,128)(2,1)} %slice_bitcast_fusion), channel_id=1, source_target_pairs={{0,8},{8,16},{16,24},{24,32},{32,40},{40,48},{48,56},{56,64},{64,7... | collective-permute-start | bytes 2949128 | tf_op jit(solution)/shard_map/ppermute | solution.py:20
  61.8 1.3 collective-permute-start.1
  63.6 7.2 %convolution_convert_fusion.4 = bf16[384,320]{0,1:T(8,128)(2,1)S(1)} fusion(bf16[384,8192]{1,0:T(8,128)(2,1)} %bitcast.61, bf16[320,8192]{1,0:T(8,128)(2,1)} %param.17), kind=kOutput, calls=%fused_computation.30 | convolution fusion | flops 2013388800 | bytes 11780096 | tf_op jit(solution)/shard_map/dot_general | solution.py:236
  70.8 11.2 %collective-permute-done.kl_ref.vl_ref = bf16[192,2560]{1,0:T(8,128)(2,1)} collective-permute-done((bf16[192,2560]{1,0:T(8,128)(2,1)}, bf16[192,2560]{1,0:T(8,128)(2,1)}, u32[]{:S(2)}, u32[]{:S(2)}) %collective-permute-start) | collective-permute-done | bytes 983072 | tf_op jit(solution)/shard_map/ppermute | solution.py:20
  82.0 4.7 %collective-permute-done.1.kh_ref.vh_ref = bf16[192,2560]{1,0:T(8,128)(2,1)} collective-permute-done((bf16[192,2560]{1,0:T(8,128)(2,1)}, bf16[192,2560]{1,0:T(8,128)(2,1)}, u32[]{:S(2)}, u32[]{:S(2)}) %collective-permute-start.1) | collective-permute-done | bytes 983072 | tf_op jit(solution)/shard_map/ppermute | solution.py:20
  86.9 1.3 convolution_convert_fusion.3
  88.2 10.8 %all-to-all-start.1 = ((bf16[32,24,384]{2,1,0:T(8,128)(2,1)}), bf16[32,24,384]{2,1,0:T(8,128)(2,1)}, u32[]{:S(2)}, u32[]{:S(2)}) async-start(bf16[32,24,384]{2,1,0:T(8,128)(2,1)} %bitcast.58), calls=%async_computation.1 | async-start | bytes 1179648 | tf_op jit(solution)/shard_map/all_to_all | solution.py:244
  99.1 16.4 %all-to-all-done.1 = bf16[32,24,384]{2,1,0:T(8,128)(2,1)} async-done(((bf16[32,24,384]{2,1,0:T(8,128)(2,1)}), bf16[32,24,384]{2,1,0:T(8,128)(2,1)}, u32[]{:S(2)}, u32[]{:S(2)}) %all-to-all-start.1) | async-done | bytes 589856 | tf_op jit(solution)/shard_map/all_to_all | solution.py:244
  116.7 1.5 fusion.17
  118.3 1.2 fusion.34
  119.5 2.5 convolution_convert_fusion
  122.1 3.5 %collective-permute-start.2 = (bf16[4,48,5120]{2,1,0:T(8,128)(2,1)}, bf16[4,48,5120]{2,1,0:T(8,128)(2,1)}, u32[]{:S(2)}, u32[]{:S(2)}) collective-permute-start(bf16[4,48,5120]{2,1,0:T(8,128)(2,1)} %convolution_convert_fusion), channel_id=1, source_target_pairs={{0,1},{1,0},{2,3},{3,2},{4,5},{5,4},{6,7},{7,6},{8,9},{9,8},{10,11... | collective-permute-start | bytes 5898248 | tf_op jit(solution)/shard_map/ppermute | solution.py:31
  125.6 3.9 %collective-permute-done.2 = bf16[4,48,5120]{2,1,0:T(8,128)(2,1)} collective-permute-done((bf16[4,48,5120]{2,1,0:T(8,128)(2,1)}, bf16[4,48,5120]{2,1,0:T(8,128)(2,1)}, u32[]{:S(2)}, u32[]{:S(2)}) %collective-permute-start.2) | collective-permute-done | bytes 1966112 | tf_op jit(solution)/shard_map/ppermute | solution.py:31
  129.5 4.1 %add_convert_fusion = bf16[4,48,5120]{2,1,0:T(8,128)(2,1)} fusion(bf16[4,48,5120]{2,1,0:T(8,128)(2,1)} %collective-permute-done.2, bf16[5120,320]{0,1:T(8,128)(2,1)S(1)} %copy-done, bf16[4,2,48,320]{3,2,1,0:T(8,128)(2,1)} %bitcast.57, s32[]{:T(128)S(6)} %select_n.166), kind=kOutput, calls=%fused_computation.3 | convolution fusion | flops 632094720 | bytes 7356420 | tf_op jit(solution)/shard_map/bmh,ih->bmi/dot_general | solution.py:263
  135.1 1.6 reshape.289
  137.0 1.2 fusion.23
  138.3 1.4 copy-done.1
  139.6 12.8 %attention_forward.1 = (bf16[192,1280]{1,0:T(8,128)(2,1)S(1)}, f32[2,192,8]{2,1,0:T(8,128)S(1)}) custom-call(bf16[1,192,3840]{2,1,0:T(8,128)(2,1)S(1)} %copy-done.1, bf16[1,192,3840]{2,1,0:T(8,128)(2,1)S(1)} %copy-done.1, bf16[1,192,3840]{2,1,0:T(8,128)(2,1)S(1)} %copy-done.1, bf16[192,2560]{1,0:T(8,128)(2,1)} %collective-permute-done.kl_ref.vl_ref, ...), custom_call_target="tpu_custom_call" | custom-call | flops 566231040 | bytes 2949120 | tf_op jit(solution)/shard_map/attention_forward/pallas_call | solution.py:161
  153.1 1.5 fusion.16
  154.6 1.5 fusion.15
  156.1 3.7 %reduce-scatter.3.cloned.1.call-done = bf16[1,48,5120]{2,1,0:T(8,128)(2,1)} async-done(((bf16[4,48,5120]{2,1,0:T(8,128)(2,1)}), bf16[1,48,5120]{2,1,0:T(8,128)(2,1)}) %reduce-scatter.3.cloned.1.call-update) | async-done | bytes 491536 | tf_op jit(solution)/shard_map/reduce_scatter | solution.py:38
  159.8 2.1 reshape.290
  161.9 1.6 fusion.22
  163.6 1.5 fusion.20
  165.8 2.7 convolution_convert_fusion.1
  169.2 5.1 %fusion.9.do_ref = bf16[192,1280]{1,0:T(8,128)(2,1)} fusion(s32[1280]{0:T(1024)S(1)} %fusion.54, bf16[192,1280]{1,0:T(8,128)(2,1)} %copy-done.11, bf16[1280,1280]{1,0:T(8,128)(2,1)} %all-gather.6.cloned.1.call-done), kind=kOutput, calls=%fused_computation.15 | convolution fusion | flops 1260421120 | bytes 4264960 | tf_op jit(solution)/shard_map/dot_general | solution.py:316
  174.3 3.5 %add_convert_fusion.1 = bf16[640,1280]{1,0:T(8,128)(2,1)} fusion(bf16[640,1280]{1,0:T(8,128)(2,1)} %collective-permute-done.3, bf16[192,640]{1,0:T(8,128)(2,1)} %fusion.15, bf16[192,1280]{1,0:T(8,128)(2,1)} %copy-done.11), kind=kOutput, calls=%fused_computation.8 | convolution fusion | flops 317030400 | bytes 4014080 | tf_op jit(solution)/shard_map/pi,pj->ij/dot_general | solution.py:303
  180.9 17.9 %attention_backward.1 = (bf16[192,1280]{1,0:T(8,128)(2,1)S(1)}, bf16[2,192,1280]{2,1,0:T(8,128)(2,1)S(1)}, f32[2,192,1280]{2,1,0:T(8,128)}, bf16[2,192,1280]{2,1,0:T(8,128)(2,1)S(1)}) custom-call(bf16[1,192,3840]{2,1,0:T(8,128)(2,1)} %v_ref.3, bf16[1,192,3840]{2,1,0:T(8,128)(2,1)} %v_ref.3, bf16[1,192,3840]{2,1,0:T(8,128)(2,1)} %v_ref.3, ...), custom_call_target="tpu_custom_call" | custom-call | flops 1415577600 | bytes 2949120 | tf_op jit(solution)/shard_map/attention_backward/pallas_call | solution.py:176
  201.4 4.1 %reduce-scatter.5.cloned.1.call-done = bf16[160,1280]{1,0:T(8,128)(2,1)} async-done(((bf16[640,1280]{1,0:T(8,128)(2,1)}), bf16[160,1280]{1,0:T(8,128)(2,1)}) %reduce-scatter.5.cloned.1.call-update) | async-done | bytes 409616 | tf_op jit(solution)/shard_map/reduce_scatter | solution.py:38
  205.5 2.0 reshape.291
  207.6 2.3 pad_maximum_fusion
  209.9 9.6 %all-to-all-start.2 = ((bf16[32,8,1280]{2,1,0:T(8,128)(2,1)}), bf16[32,8,1280]{2,1,0:T(8,128)(2,1)}, u32[]{:S(2)}, u32[]{:S(2)}) async-start(bf16[32,8,1280]{2,1,0:T(8,128)(2,1)} %pad_maximum_fusion), calls=%async_computation.4 | async-start | bytes 1310720 | tf_op jit(solution)/shard_map/all_to_all | solution.py:330
  219.4 4.1 %collective-permute-start.4 = (bf16[2,192,1280]{2,1,0:T(8,128)(2,1)}, bf16[2,192,1280]{2,1,0:T(8,128)(2,1)}, u32[]{:S(2)}, u32[]{:S(2)}) collective-permute-start(bf16[2,192,1280]{2,1,0:T(8,128)(2,1)} %copy-done.10), channel_id=1, source_target_pairs={{0,8},{8,16},{16,24},{24,32},{32,40},{40,48},{48,56},{56,64},{64,7... | collective-permute-start | bytes 2949128 | tf_op jit(solution)/shard_map/ppermute | solution.py:20
  223.5 1.3 collective-permute-start.5
  224.8 23.9 %collective-permute-done.4 = bf16[2,192,1280]{2,1,0:T(8,128)(2,1)} collective-permute-done((bf16[2,192,1280]{2,1,0:T(8,128)(2,1)}, bf16[2,192,1280]{2,1,0:T(8,128)(2,1)}, u32[]{:S(2)}, u32[]{:S(2)}) %collective-permute-start.4) | collective-permute-done | bytes 983072 | tf_op jit(solution)/shard_map/ppermute | solution.py:20
  248.7 3.8 %collective-permute-done.5 = bf16[2,192,1280]{2,1,0:T(8,128)(2,1)} collective-permute-done((bf16[2,192,1280]{2,1,0:T(8,128)(2,1)}, bf16[2,192,1280]{2,1,0:T(8,128)(2,1)}, u32[]{:S(2)}, u32[]{:S(2)}) %collective-permute-start.5) | collective-permute-done | bytes 983072 | tf_op jit(solution)/shard_map/ppermute | solution.py:20
  252.5 1.2 convert_reduce_fusion
  253.8 14.0 %all-gather.2 = bf16[64,1280]{1,0:T(8,128)(2,1)S(1)} all-gather(bf16[8,1280]{1,0:T(8,128)(2,1)S(1)} %pad_maximum_fusion.1), channel_id=4, replica_groups=mesh['cp'=32,'dp'=8] {'dp'}, dimensions={0}, use_global_device_ids=true | all-gather | bytes 184320 | tf_op jit(solution)/shard_map/all_gather | solution.py:338
  269.3 1.7 reshape.292
  270.9 2.4 add_convert_fusion.2
  273.5 1.2 maximum_bitcast_fusion
  (83 shorter events, 16.0 us)
Async XLA Ops:
  7.2 112.4 %copy-start = (bf16[5120,320]{0,1:T(8,128)(2,1)S(1)}, bf16[5120,320]{0,1:T(8,128)(2,1)}, u32[]{:S(2)}) copy-start(bf16[5120,320]{0,1:T(8,128)(2,1)} %param.16) | copy-start | bytes 9830404
  7.2 35.3 %copy-start.16 = (s32[1,48]{1,0:T(1,128)S(1)}, s32[1,48]{1,0:T(1,128)}, u32[]{:S(2)}) copy-start(s32[1,48]{1,0:T(1,128)} %param.11) | copy-start | bytes 580
  7.2 50.5 %all-gather.8.cloned.1.call-start = ((), (), s32[]{:S(2)}) async-start(), calls=%async_computation.8 | async-start | bytes 7077888 | tf_op jit(solution)/shard_map/all_gather | solution.py:208
  9.8 30.7 %all-to-all-start = ((bf16[32,5,1280]{2,1,0:T(8,128)(2,1)}), bf16[32,5,1280]{2,1,0:T(8,128)(2,1)}, u32[]{:S(2)}, u32[]{:S(2)}) async-start(bf16[32,5,1280]{2,1,0:T(8,128)(2,1)} %broadcast_in_dim.38), calls=%async_computation | async-start | bytes 1310720 | tf_op jit(solution)/shard_map/all_to_all | solution.py:212
  21.8 93.8 %all-gather.6.cloned.1.call-start = ((), (), s32[]{:S(2)}) async-start(), calls=%async_computation.5 | async-start | bytes 3686400 | tf_op jit(solution)/shard_map/all_gather | solution.py:224
  57.7 24.3 %collective-permute-start = (bf16[192,2560]{1,0:T(8,128)(2,1)}, bf16[192,2560]{1,0:T(8,128)(2,1)}, u32[]{:S(2)}, u32[]{:S(2)}) collective-permute-start(bf16[192,2560]{1,0:T(8,128)(2,1)} %slice_bitcast_fusion), channel_id=1, source_target_pairs={{0,8},{8,16},{16,24},{24,32},{32,40},{40,48},{48,56},{56,64},{64,7... | collective-permute-start | bytes 2949128 | tf_op jit(solution)/shard_map/ppermute | solution.py:20
  61.8 25.0 %collective-permute-start.1 = (bf16[192,2560]{1,0:T(8,128)(2,1)}, bf16[192,2560]{1,0:T(8,128)(2,1)}, u32[]{:S(2)}, u32[]{:S(2)}) collective-permute-start(bf16[192,2560]{1,0:T(8,128)(2,1)} %slice_bitcast_fusion), channel_id=1, source_target_pairs={{8,0},{16,8},{24,16},{32,24},{40,32},{48,40},{56,48},{64,56},{72,6... | collective-permute-start | bytes 2949128 | tf_op jit(solution)/shard_map/ppermute | solution.py:20
  88.2 27.3 %all-to-all-start.1 = ((bf16[32,24,384]{2,1,0:T(8,128)(2,1)}), bf16[32,24,384]{2,1,0:T(8,128)(2,1)}, u32[]{:S(2)}, u32[]{:S(2)}) async-start(bf16[32,24,384]{2,1,0:T(8,128)(2,1)} %bitcast.58), calls=%async_computation.1 | async-start | bytes 1179648 | tf_op jit(solution)/shard_map/all_to_all | solution.py:244
  99.0 60.8 %reduce-scatter.3.cloned.1.call-start = ((), (), s32[]{:S(2)}) async-start(), calls=%async_computation.6 | async-start | bytes 2457600 | tf_op jit(solution)/shard_map/reduce_scatter | solution.py:38
  119.5 2.5 copy-start.13
  122.1 7.4 %collective-permute-start.2 = (bf16[4,48,5120]{2,1,0:T(8,128)(2,1)}, bf16[4,48,5120]{2,1,0:T(8,128)(2,1)}, u32[]{:S(2)}, u32[]{:S(2)}) collective-permute-start(bf16[4,48,5120]{2,1,0:T(8,128)(2,1)} %convolution_convert_fusion), channel_id=1, source_target_pairs={{0,1},{1,0},{2,3},{3,2},{4,5},{5,4},{6,7},{7,6},{8,9},{9,8},{10,11... | collective-permute-start | bytes 5898248 | tf_op jit(solution)/shard_map/ppermute | solution.py:31
  125.6 8.3 %copy-start.15 = (s32[1,1536]{1,0:T(1,128)S(1)}, s32[1,1536]{1,0:T(1,128)}, u32[]{:S(2)}) copy-start(s32[1,1536]{1,0:T(1,128)} %param.12) | copy-start | bytes 18436
  133.6 71.9 %reduce-scatter.5.cloned.1.call-start = ((), (), s32[]{:S(2)}) async-start(), calls=%async_computation.7 | async-start | bytes 2048000 | tf_op jit(solution)/shard_map/reduce_scatter | solution.py:38
  138.3 1.4 copy-start.1
  152.4 0.7 copy-start.7
  153.1 1.5 copy-start.4
  153.1 8.8 %copy-start.14 = (f32[1280]{0:T(1024)S(1)}, f32[1280]{0:T(1024)}, u32[]{:S(2)}) copy-start(f32[1280]{0:T(1024)} %param.14) | copy-start | bytes 15364
  165.0 0.8 copy-start.11
  168.5 5.7 %collective-permute-start.3 = (bf16[640,1280]{1,0:T(8,128)(2,1)}, bf16[640,1280]{1,0:T(8,128)(2,1)}, u32[]{:S(2)}, u32[]{:S(2)}) collective-permute-start(bf16[640,1280]{1,0:T(8,128)(2,1)} %convolution_convert_fusion.1), channel_id=1, source_target_pairs={{0,1},{1,0},{2,3},{3,2},{4,5},{5,4},{6,7},{7,6},{8,9},{9,8},{10,11... | collective-permute-start | bytes 4915208 | tf_op jit(solution)/shard_map/ppermute | solution.py:31
  177.9 1.0 copy-start.5
  178.9 1.0 copy-start.6
  179.9 0.9 copy-start.8
  198.7 0.8 copy-start.2
  199.5 0.9 copy-start.9
  200.5 1.0 copy-start.10
  209.9 42.6 %all-to-all-start.2 = ((bf16[32,8,1280]{2,1,0:T(8,128)(2,1)}), bf16[32,8,1280]{2,1,0:T(8,128)(2,1)}, u32[]{:S(2)}, u32[]{:S(2)}) async-start(bf16[32,8,1280]{2,1,0:T(8,128)(2,1)} %pad_maximum_fusion), calls=%async_computation.4 | async-start | bytes 1310720 | tf_op jit(solution)/shard_map/all_to_all | solution.py:330
  219.4 29.3 %collective-permute-start.4 = (bf16[2,192,1280]{2,1,0:T(8,128)(2,1)}, bf16[2,192,1280]{2,1,0:T(8,128)(2,1)}, u32[]{:S(2)}, u32[]{:S(2)}) collective-permute-start(bf16[2,192,1280]{2,1,0:T(8,128)(2,1)} %copy-done.10), channel_id=1, source_target_pairs={{0,8},{8,16},{16,24},{24,32},{32,40},{40,48},{48,56},{56,64},{64,7... | collective-permute-start | bytes 2949128 | tf_op jit(solution)/shard_map/ppermute | solution.py:20
  223.5 29.0 %collective-permute-start.5 = (bf16[2,192,1280]{2,1,0:T(8,128)(2,1)}, bf16[2,192,1280]{2,1,0:T(8,128)(2,1)}, u32[]{:S(2)}, u32[]{:S(2)}) collective-permute-start(bf16[2,192,1280]{2,1,0:T(8,128)(2,1)} %copy-done.9), channel_id=1, source_target_pairs={{8,0},{16,8},{24,16},{32,24},{40,32},{48,40},{56,48},{64,56},{72,6... | collective-permute-start | bytes 2949128 | tf_op jit(solution)/shard_map/ppermute | solution.py:20
  267.9 0.7 copy-start.12
  270.9 2.5 copy-start.3
Sparse Core Ops, SparseCore 0:
  9.9 47.7 all-gather.7
  60.1 31.0 all-gather.5
  133.7 26.0 reduce-scatter.2
  177.9 27.5 reduce-scatter.4

commit v3 on v2

--- a/solution.py
+++ b/solution.py
@@ -234,7 +234,6 @@
     slots = shards * batches * slot_count
     pick = (jnp.arange(slots, dtype=jnp.int32)[:, None] == slot).astype(narrow)
     d_rows = jnp.dot(gathered, w_out.T, preferred_element_type=single).astype(narrow)
-    d_rows, low, high = lax.optimization_barrier((d_rows, low, high))
     tags = jnp.where(
         jnp.arange(packed_width - hidden)[None, :] == 0, place + 1, 0
     ).astype(narrow)
@@ -248,7 +247,7 @@
         concat_axis=0,
         tiled=True,
     ).reshape(slots, packed_width)
-    arrived, full_proj = lax.optimization_barrier((arrived, full_proj))
+    arrived, full_proj, low, high = lax.optimization_barrier((arrived, full_proj, low, high))
     tag_row = arrived[:, hidden].astype(jnp.int32).reshape(1, slots)
     slot_batch = (jnp.arange(slots, dtype=jnp.int32) // slot_count % batches)[None, :]
     home = jnp.where(tag_row > 0, slot_batch * row_count + tag_row - 1, -1)
@@ -328,7 +327,6 @@
         axis=1,
     )
     per_shard = lax.all_to_all(spread, "cp", split_axis=0, concat_axis=0, tiled=True)
-    per_shard, from_prev, from_next = lax.optimization_barrier((per_shard, from_prev, from_next))
     d_pairs = (d_own + from_prev.astype(single) + from_next.astype(single)).astype(narrow)
     d_qkv = jnp.concatenate([d_query, d_pairs[0], d_pairs[1]], axis=1)
     totals = jnp.sum(per_shard.astype(single), axis=0)

time: 286 us -> 275 us (0.962); the launches traced: 281 us -> 274 us
  waiting for transfers between devices: 91.7 us -> 85.6 us
    all_to_all x1, waiting for transfers between devices: 0.01 us -> 18.5 us  [local(): lax.all_to_all(spread, 'cp', split_axis=0, concat_axis=0, tiled=True)]
    all_to_all x1, waiting for transfers between devices: 16.4 us -> 0.01 us  [local(): lax.all_to_all(outgoing.reshape(shards, batches * slot_count, packed_widt...]
    ppermute x4, waiting for transfers between devices: 43.7 us -> 32.8 us  [from_behind(): return lax.ppermute(block, axis, route)]
    unnamed x37 -> x33, local copies, waits for them, and re-layouts: 10.7 us -> 8.78 us
  transfers between devices with their start and end apart: 13 -> 13, of which waited for: 10 -> 9; matrix products, arithmetic and copies ran while one was open for 10% -> 14% of each run, Pallas kernels for 11% -> 11%
where the time goes in v3:
time: 275 us; the launch traced here: 274 us
  waiting for transfers between devices  85.6 us (31%)
  starting transfers between devices  45.9 us (17%)
  matrix products  31.1 us (11%)
  Pallas kernels  30.7 us (11%)
  blocking collectives  26.5 us (10%)
  local copies, waits for them, and re-layouts  24.1 us (9%)
  other arithmetic  15.1 us (5%)
  between operations  14.8 us (5%)
    ppermute x4, waiting for transfers between devices, from_behind(): return lax.ppermute(block, axis, route)  32.8 us
    all_to_all x1, waiting for transfers between devices, local(): lax.all_to_all(spread, 'cp', split_axis=0, concat_axis=0, tiled=True)  18.5 us
    pallas_call x1, Pallas kernels, backward(): pl.pallas_call(backward_kernel, grid=(groups,), in_specs=own + halo + ids...  18 us
    all_gather x1, blocking collectives, local(): whole = lax.all_gather(own_rows, 'dp', axis=0).astype(single)  16.3 us
    all_to_all x1, waiting for transfers between devices, local(): lax.all_to_all(jnp.broadcast_to(own_proj[None], (shards, part, width)), '...  14.5 us
    pallas_call x1, Pallas kernels, attention_calls(): pl.pallas_call(forward_kernel, grid=(groups,), in_specs=own + halo + ids,...  12.7 us
    all_to_all x1, starting transfers between devices, local(): lax.all_to_all(jnp.broadcast_to(own_proj[None], (shards, part, width)), '...  12 us
    ppermute x4, starting transfers between devices, from_behind(): return lax.ppermute(block, axis, route)  11.6 us
  transfers between devices with their start and end apart: 13, of which 9 were waited for; matrix products, arithmetic and copies ran while one was open for 14% of the time, Pallas kernels for 11%

profile of v3, /device:TPU:1, one launch (start us, length us, event | category | flops | bytes accessed | tf_op | source)
XLA Modules:
  0.0 273.9 jit_solution(16354386340274586019)
XLA Ops:
  9.8 12.0 %all-to-all-start = ((bf16[32,5,1280]{2,1,0:T(8,128)(2,1)}), bf16[32,5,1280]{2,1,0:T(8,128)(2,1)}, u32[]{:S(2)}, u32[]{:S(2)}) async-start(bf16[32,5,1280]{2,1,0:T(8,128)(2,1)} %broadcast_in_dim.38), calls=%async_computation | async-start | bytes 1310720 | tf_op jit(solution)/shard_map/all_to_all | solution.py:212
  21.8 1.3 dynamic-slice
  23.7 2.2 slice_bitcast_fusion
  25.9 14.5 %all-to-all-done = bf16[32,5,1280]{2,1,0:T(8,128)(2,1)} async-done(((bf16[32,5,1280]{2,1,0:T(8,128)(2,1)}), bf16[32,5,1280]{2,1,0:T(8,128)(2,1)}, u32[]{:S(2)}, u32[]{:S(2)}) %all-to-all-start) | async-done | bytes 409632 | tf_op jit(solution)/shard_map/all_to_all | solution.py:212
  40.4 2.0 reshape.284
  42.6 10.3 %all-reduce = s32[384]{0:T(512)S(1)} all-reduce(s32[384]{0:T(512)S(1)} %dynamic-update-slice), channel_id=3, replica_groups=mesh['cp'=32,'dp'=8] {'dp'}, use_global_device_ids=true, to_apply=%add | all-reduce | flops 384 | bytes 3072
  53.0 4.7 %all-gather.8.cloned.1.call-done = bf16[1,384,8192]{2,1,0:T(8,128)(2,1)} async-done(((bf16[1,48,8192]{2,1,0:T(8,128)(2,1)}), bf16[1,384,8192]{2,1,0:T(8,128)(2,1)}) %all-gather.8.cloned.1.call-update) | async-done | bytes 6291472 | tf_op jit(solution)/shard_map/all_gather | solution.py:208
  58.4 7.2 %convolution_convert_fusion.4 = bf16[384,320]{0,1:T(8,128)(2,1)S(1)} fusion(bf16[384,8192]{1,0:T(8,128)(2,1)} %bitcast.61, bf16[320,8192]{1,0:T(8,128)(2,1)} %param.17), kind=kOutput, calls=%fused_computation.30 | convolution fusion | flops 2013388800 | bytes 11780096 | tf_op jit(solution)/shard_map/dot_general | solution.py:236
  65.5 1.4 convolution_convert_fusion.3
  66.9 9.6 %all-to-all-start.1 = ((bf16[32,24,384]{2,1,0:T(8,128)(2,1)}), bf16[32,24,384]{2,1,0:T(8,128)(2,1)}, u32[]{:S(2)}, u32[]{:S(2)}) async-start(bf16[32,24,384]{2,1,0:T(8,128)(2,1)} %bitcast.58), calls=%async_computation.1 | async-start | bytes 1179648 | tf_op jit(solution)/shard_map/all_to_all | solution.py:243
  76.6 4.0 %collective-permute-start = (bf16[192,2560]{1,0:T(8,128)(2,1)}, bf16[192,2560]{1,0:T(8,128)(2,1)}, u32[]{:S(2)}, u32[]{:S(2)}) collective-permute-start(bf16[192,2560]{1,0:T(8,128)(2,1)} %slice_bitcast_fusion), channel_id=1, source_target_pairs={{0,8},{8,16},{16,24},{24,32},{32,40},{40,48},{48,56},{56,64},{64,7... | collective-permute-start | bytes 2949128 | tf_op jit(solution)/shard_map/ppermute | solution.py:20
  80.6 1.3 collective-permute-start.1
  81.9 23.8 %collective-permute-done.kl_ref.vl_ref = bf16[192,2560]{1,0:T(8,128)(2,1)} collective-permute-done((bf16[192,2560]{1,0:T(8,128)(2,1)}, bf16[192,2560]{1,0:T(8,128)(2,1)}, u32[]{:S(2)}, u32[]{:S(2)}) %collective-permute-start) | collective-permute-done | bytes 983072 | tf_op jit(solution)/shard_map/ppermute | solution.py:20
  105.7 3.2 %collective-permute-done.1.kh_ref.vh_ref = bf16[192,2560]{1,0:T(8,128)(2,1)} collective-permute-done((bf16[192,2560]{1,0:T(8,128)(2,1)}, bf16[192,2560]{1,0:T(8,128)(2,1)}, u32[]{:S(2)}, u32[]{:S(2)}) %collective-permute-start.1) | collective-permute-done | bytes 983072 | tf_op jit(solution)/shard_map/ppermute | solution.py:20
  108.9 1.2 convert_reduce_fusion.1
  110.1 1.5 fusion.17
  111.7 1.2 fusion.34
  112.9 2.5 convolution_convert_fusion
  115.5 1.2 collective-permute-start.2
  116.7 3.9 %collective-permute-done.2 = bf16[4,48,5120]{2,1,0:T(8,128)(2,1)} collective-permute-done((bf16[4,48,5120]{2,1,0:T(8,128)(2,1)}, bf16[4,48,5120]{2,1,0:T(8,128)(2,1)}, u32[]{:S(2)}, u32[]{:S(2)}) %collective-permute-start.2) | collective-permute-done | bytes 1966112 | tf_op jit(solution)/shard_map/ppermute | solution.py:31
  120.6 4.1 %add_convert_fusion = bf16[4,48,5120]{2,1,0:T(8,128)(2,1)} fusion(bf16[4,48,5120]{2,1,0:T(8,128)(2,1)} %collective-permute-done.2, bf16[5120,320]{0,1:T(8,128)(2,1)S(1)} %copy-done, bf16[4,2,48,320]{3,2,1,0:T(8,128)(2,1)} %bitcast.57, s32[]{:T(128)S(6)} %select_n.166), kind=kOutput, calls=%fused_computation.3 | convolution fusion | flops 632094720 | bytes 7356420 | tf_op jit(solution)/shard_map/bmh,ih->bmi/dot_general | solution.py:262
  126.2 1.6 reshape.289
  128.2 1.2 fusion.23
  129.4 1.4 copy-done.1
  130.8 12.7 %attention_forward.1 = (bf16[192,1280]{1,0:T(8,128)(2,1)S(1)}, f32[2,192,8]{2,1,0:T(8,128)S(1)}) custom-call(bf16[1,192,3840]{2,1,0:T(8,128)(2,1)S(1)} %copy-done.1, bf16[1,192,3840]{2,1,0:T(8,128)(2,1)S(1)} %copy-done.1, bf16[1,192,3840]{2,1,0:T(8,128)(2,1)S(1)} %copy-done.1, bf16[192,2560]{1,0:T(8,128)(2,1)} %collective-permute-done.kl_ref.vl_ref, ...), custom_call_target="tpu_custom_call" | custom-call | flops 566231040 | bytes 2949120 | tf_op jit(solution)/shard_map/attention_forward/pallas_call | solution.py:161
  144.1 1.5 fusion.16
  145.7 1.5 fusion.15
  147.2 10.4 %reduce-scatter.3.cloned.1.call-done = bf16[1,48,5120]{2,1,0:T(8,128)(2,1)} async-done(((bf16[4,48,5120]{2,1,0:T(8,128)(2,1)}), bf16[1,48,5120]{2,1,0:T(8,128)(2,1)}) %reduce-scatter.3.cloned.1.call-update) | async-done | bytes 491536 | tf_op jit(solution)/shard_map/reduce_scatter | solution.py:38
  157.5 2.1 reshape.290
  159.7 1.6 fusion.22
  161.3 1.5 fusion.20
  163.5 2.7 %convolution_convert_fusion.1 = bf16[640,1280]{1,0:T(8,128)(2,1)} fusion(bf16[192,640]{1,0:T(8,128)(2,1)} %fusion.16, bf16[192,1280]{1,0:T(8,128)(2,1)S(1)} %fusion.20), kind=kOutput, calls=%fused_computation.13 | convolution fusion | flops 315392000 | bytes 2375680 | tf_op jit(solution)/shard_map/pi,pj->ij/dot_general | solution.py:302
  166.9 5.1 %fusion.9.do_ref = bf16[192,1280]{1,0:T(8,128)(2,1)} fusion(s32[1280]{0:T(1024)S(1)} %fusion.54, bf16[192,1280]{1,0:T(8,128)(2,1)} %copy-done.9, bf16[1280,1280]{1,0:T(8,128)(2,1)} %all-gather.6.cloned.1.call-done), kind=kOutput, calls=%fused_computation.15 | convolution fusion | flops 1260421120 | bytes 4264960 | tf_op jit(solution)/shard_map/dot_general | solution.py:315
  172.1 3.5 %add_convert_fusion.1 = bf16[640,1280]{1,0:T(8,128)(2,1)} fusion(bf16[640,1280]{1,0:T(8,128)(2,1)} %collective-permute-done.3, bf16[192,640]{1,0:T(8,128)(2,1)} %fusion.15, bf16[192,1280]{1,0:T(8,128)(2,1)} %copy-done.9), kind=kOutput, calls=%fused_computation.8 | convolution fusion | flops 317030400 | bytes 4014080 | tf_op jit(solution)/shard_map/pi,pj->ij/dot_general | solution.py:302
  178.6 18.0 %attention_backward.1 = (bf16[192,1280]{1,0:T(8,128)(2,1)S(1)}, bf16[2,192,1280]{2,1,0:T(8,128)(2,1)}, f32[2,192,1280]{2,1,0:T(8,128)}, bf16[2,192,1280]{2,1,0:T(8,128)(2,1)}) custom-call(bf16[1,192,3840]{2,1,0:T(8,128)(2,1)} %v_ref.3, bf16[1,192,3840]{2,1,0:T(8,128)(2,1)} %v_ref.3, bf16[1,192,3840]{2,1,0:T(8,128)(2,1)} %v_ref.3, ...), custom_call_target="tpu_custom_call" | custom-call | flops 1415577600 | bytes 2949120 | tf_op jit(solution)/shard_map/attention_backward/pallas_call | solution.py:176
  197.4 1.3 collective-permute-start.5
  198.7 5.0 %collective-permute-start.4 = (bf16[2,192,1280]{2,1,0:T(8,128)(2,1)}, bf16[2,192,1280]{2,1,0:T(8,128)(2,1)}, u32[]{:S(2)}, u32[]{:S(2)}) collective-permute-start(bf16[2,192,1280]{2,1,0:T(8,128)(2,1)} %get-tuple-element.47), channel_id=1, source_target_pairs={{0,8},{8,16},{16,24},{24,32},{32,40},{40,48},{48,56},{56,64},{64,7... | collective-permute-start | bytes 2949128 | tf_op jit(solution)/shard_map/ppermute | solution.py:20
  203.8 2.0 reshape.291
  205.9 2.3 pad_maximum_fusion
  208.1 10.5 %all-to-all-start.2 = ((bf16[32,8,1280]{2,1,0:T(8,128)(2,1)}), bf16[32,8,1280]{2,1,0:T(8,128)(2,1)}, u32[]{:S(2)}, u32[]{:S(2)}) async-start(bf16[32,8,1280]{2,1,0:T(8,128)(2,1)} %pad_maximum_fusion), calls=%async_computation.4 | async-start | bytes 1310720 | tf_op jit(solution)/shard_map/all_to_all | solution.py:329
  218.6 4.6 %collective-permute-done.5 = bf16[2,192,1280]{2,1,0:T(8,128)(2,1)} collective-permute-done((bf16[2,192,1280]{2,1,0:T(8,128)(2,1)}, bf16[2,192,1280]{2,1,0:T(8,128)(2,1)}, u32[]{:S(2)}, u32[]{:S(2)}) %collective-permute-start.5) | collective-permute-done | bytes 983072 | tf_op jit(solution)/shard_map/ppermute | solution.py:20
  223.2 1.2 collective-permute-done.4
  224.4 2.4 add_convert_fusion.2
  226.9 1.2 maximum_bitcast_fusion
  228.1 18.5 %all-to-all-done.2 = bf16[32,8,1280]{2,1,0:T(8,128)(2,1)} async-done(((bf16[32,8,1280]{2,1,0:T(8,128)(2,1)}), bf16[32,8,1280]{2,1,0:T(8,128)(2,1)}, u32[]{:S(2)}, u32[]{:S(2)}) %all-to-all-start.2) | async-done | bytes 655392 | tf_op jit(solution)/shard_map/all_to_all | solution.py:329
  246.7 1.2 convert_reduce_fusion
  247.9 16.3 %all-gather.2 = bf16[64,1280]{1,0:T(8,128)(2,1)S(1)} all-gather(bf16[8,1280]{1,0:T(8,128)(2,1)S(1)} %pad_maximum_fusion.1), channel_id=4, replica_groups=mesh['cp'=32,'dp'=8] {'dp'}, dimensions={0}, use_global_device_ids=true | all-gather | bytes 184320 | tf_op jit(solution)/shard_map/all_gather | solution.py:336
  265.6 1.7 reshape.292
  (79 shorter events, 13.0 us)
Async XLA Ops:
  7.2 105.8 %copy-start = (bf16[5120,320]{0,1:T(8,128)(2,1)S(1)}, bf16[5120,320]{0,1:T(8,128)(2,1)}, u32[]{:S(2)}) copy-start(bf16[5120,320]{0,1:T(8,128)(2,1)} %param.16) | copy-start | bytes 9830404
  7.2 35.3 %copy-start.14 = (s32[1,48]{1,0:T(1,128)S(1)}, s32[1,48]{1,0:T(1,128)}, u32[]{:S(2)}) copy-start(s32[1,48]{1,0:T(1,128)} %param.11) | copy-start | bytes 580
  7.2 50.5 %all-gather.8.cloned.1.call-start = ((), (), s32[]{:S(2)}) async-start(), calls=%async_computation.8 | async-start | bytes 7077888 | tf_op jit(solution)/shard_map/all_gather | solution.py:208
  9.8 30.7 %all-to-all-start = ((bf16[32,5,1280]{2,1,0:T(8,128)(2,1)}), bf16[32,5,1280]{2,1,0:T(8,128)(2,1)}, u32[]{:S(2)}, u32[]{:S(2)}) async-start(bf16[32,5,1280]{2,1,0:T(8,128)(2,1)} %broadcast_in_dim.38), calls=%async_computation | async-start | bytes 1310720 | tf_op jit(solution)/shard_map/all_to_all | solution.py:212
  21.7 87.2 %all-gather.6.cloned.1.call-start = ((), (), s32[]{:S(2)}) async-start(), calls=%async_computation.5 | async-start | bytes 3686400 | tf_op jit(solution)/shard_map/all_gather | solution.py:224
  66.9 42.0 %all-to-all-start.1 = ((bf16[32,24,384]{2,1,0:T(8,128)(2,1)}), bf16[32,24,384]{2,1,0:T(8,128)(2,1)}, u32[]{:S(2)}, u32[]{:S(2)}) async-start(bf16[32,24,384]{2,1,0:T(8,128)(2,1)} %bitcast.58), calls=%async_computation.1 | async-start | bytes 1179648 | tf_op jit(solution)/shard_map/all_to_all | solution.py:243
  76.6 81.0 %reduce-scatter.3.cloned.1.call-start = ((), (), s32[]{:S(2)}) async-start(), calls=%async_computation.6 | async-start | bytes 2457600 | tf_op jit(solution)/shard_map/reduce_scatter | solution.py:38
  76.6 29.1 %collective-permute-start = (bf16[192,2560]{1,0:T(8,128)(2,1)}, bf16[192,2560]{1,0:T(8,128)(2,1)}, u32[]{:S(2)}, u32[]{:S(2)}) collective-permute-start(bf16[192,2560]{1,0:T(8,128)(2,1)} %slice_bitcast_fusion), channel_id=1, source_target_pairs={{0,8},{8,16},{16,24},{24,32},{32,40},{40,48},{48,56},{56,64},{64,7... | collective-permute-start | bytes 2949128 | tf_op jit(solution)/shard_map/ppermute | solution.py:20
  80.6 28.3 %collective-permute-start.1 = (bf16[192,2560]{1,0:T(8,128)(2,1)}, bf16[192,2560]{1,0:T(8,128)(2,1)}, u32[]{:S(2)}, u32[]{:S(2)}) collective-permute-start(bf16[192,2560]{1,0:T(8,128)(2,1)} %slice_bitcast_fusion), channel_id=1, source_target_pairs={{8,0},{16,8},{24,16},{32,24},{40,32},{48,40},{56,48},{64,56},{72,6... | collective-permute-start | bytes 2949128 | tf_op jit(solution)/shard_map/ppermute | solution.py:20
  112.9 2.5 copy-start.11
  115.5 5.2 %collective-permute-start.2 = (bf16[4,48,5120]{2,1,0:T(8,128)(2,1)}, bf16[4,48,5120]{2,1,0:T(8,128)(2,1)}, u32[]{:S(2)}, u32[]{:S(2)}) collective-permute-start(bf16[4,48,5120]{2,1,0:T(8,128)(2,1)} %convolution_convert_fusion), channel_id=1, source_target_pairs={{0,1},{1,0},{2,3},{3,2},{4,5},{5,4},{6,7},{7,6},{8,9},{9,8},{10,11... | collective-permute-start | bytes 5898248 | tf_op jit(solution)/shard_map/ppermute | solution.py:31
  116.7 8.3 %copy-start.13 = (s32[1,1536]{1,0:T(1,128)S(1)}, s32[1,1536]{1,0:T(1,128)}, u32[]{:S(2)}) copy-start(s32[1,1536]{1,0:T(1,128)} %param.12) | copy-start | bytes 18436
  124.8 79.0 %reduce-scatter.5.cloned.1.call-start = ((), (), s32[]{:S(2)}) async-start(), calls=%async_computation.7 | async-start | bytes 2048000 | tf_op jit(solution)/shard_map/reduce_scatter | solution.py:38
  129.4 1.4 copy-start.1
  143.4 0.7 copy-start.7
  144.1 1.5 copy-start.4
  144.1 15.5 %copy-start.12 = (f32[1280]{0:T(1024)S(1)}, f32[1280]{0:T(1024)}, u32[]{:S(2)}) copy-start(f32[1280]{0:T(1024)} %param.14) | copy-start | bytes 15364
  162.8 0.8 copy-start.9
  166.3 5.8 %collective-permute-start.3 = (bf16[640,1280]{1,0:T(8,128)(2,1)}, bf16[640,1280]{1,0:T(8,128)(2,1)}, u32[]{:S(2)}, u32[]{:S(2)}) collective-permute-start(bf16[640,1280]{1,0:T(8,128)(2,1)} %convolution_convert_fusion.1), channel_id=1, source_target_pairs={{0,1},{1,0},{2,3},{3,2},{4,5},{5,4},{6,7},{7,6},{8,9},{9,8},{10,11... | collective-permute-start | bytes 4915208 | tf_op jit(solution)/shard_map/ppermute | solution.py:31
  175.6 1.0 copy-start.5
  176.6 1.0 copy-start.6
  177.7 0.9 copy-start.8
  196.6 0.8 copy-start.2
  197.4 25.8 %collective-permute-start.5 = (bf16[2,192,1280]{2,1,0:T(8,128)(2,1)}, bf16[2,192,1280]{2,1,0:T(8,128)(2,1)}, u32[]{:S(2)}, u32[]{:S(2)}) collective-permute-start(bf16[2,192,1280]{2,1,0:T(8,128)(2,1)} %get-tuple-element.48), channel_id=1, source_target_pairs={{8,0},{16,8},{24,16},{32,24},{40,32},{48,40},{56,48},{64,56},{72,6... | collective-permute-start | bytes 2949128 | tf_op jit(solution)/shard_map/ppermute | solution.py:20
  198.7 25.7 %collective-permute-start.4 = (bf16[2,192,1280]{2,1,0:T(8,128)(2,1)}, bf16[2,192,1280]{2,1,0:T(8,128)(2,1)}, u32[]{:S(2)}, u32[]{:S(2)}) collective-permute-start(bf16[2,192,1280]{2,1,0:T(8,128)(2,1)} %get-tuple-element.47), channel_id=1, source_target_pairs={{0,8},{8,16},{16,24},{24,32},{32,40},{40,48},{48,56},{56,64},{64,7... | collective-permute-start | bytes 2949128 | tf_op jit(solution)/shard_map/ppermute | solution.py:20
  208.1 38.5 %all-to-all-start.2 = ((bf16[32,8,1280]{2,1,0:T(8,128)(2,1)}), bf16[32,8,1280]{2,1,0:T(8,128)(2,1)}, u32[]{:S(2)}, u32[]{:S(2)}) async-start(bf16[32,8,1280]{2,1,0:T(8,128)(2,1)} %pad_maximum_fusion), calls=%async_computation.4 | async-start | bytes 1310720 | tf_op jit(solution)/shard_map/all_to_all | solution.py:329
  224.4 2.5 copy-start.3
  264.3 0.7 copy-start.10
Sparse Core Ops, SparseCore 0:
  9.9 47.7 all-gather.7
  60.1 31.0 all-gather.5
  124.9 32.6 reduce-scatter.2
  175.7 27.4 reduce-scatter.4

commit v4 on v3

--- a/solution.py
+++ b/solution.py
@@ -205,7 +205,9 @@
     slot_count = 2 * row_count // shards
     rows = batches * row_count
     packed_width = -(-(hidden + 1) // 128) * 128
-    gathered = lax.all_gather(llm_grads[0], "dp", axis=0, tiled=True)
+    half = llm_grads.shape[2] // 2
+    left = lax.all_gather(llm_grads[0, :, :half], "dp", axis=0, tiled=True)
+    right = lax.all_gather(llm_grads[0, :, half:], "dp", axis=0, tiled=True)
     share = w_proj.shape[0]
     part = share // batches
     own_proj = lax.dynamic_slice_in_dim(w_proj, lax.axis_index("dp") * part, part, 0)
@@ -220,7 +222,7 @@
         (proj_parts, qkv[0, :, width:], llm_owner[0])
     )
     owners = lax.all_gather(own_owners, "dp", axis=0)
-    gathered, proj_parts, owners = lax.optimization_barrier((gathered, proj_parts, owners))
+    right, proj_parts, owners = lax.optimization_barrier((right, proj_parts, owners))
     full_proj = lax.all_gather(proj_parts, "dp", axis=0, tiled=True)
     low = from_behind(key_values, "cp", 1)
     high = from_behind(key_values, "cp", -1)
@@ -233,7 +235,9 @@
     slot = ((target * batches + batch_of) * slot_count + rank).reshape(1, rows)
     slots = shards * batches * slot_count
     pick = (jnp.arange(slots, dtype=jnp.int32)[:, None] == slot).astype(narrow)
-    d_rows = jnp.dot(gathered, w_out.T, preferred_element_type=single).astype(narrow)
+    left_rows = jnp.dot(left, w_out[:, :half].T, preferred_element_type=single)
+    right_rows = jnp.dot(right, w_out[:, half:].T, preferred_element_type=single)
+    d_rows = (left_rows + right_rows).astype(narrow)
     tags = jnp.where(
         jnp.arange(packed_width - hidden)[None, :] == 0, place + 1, 0
     ).astype(narrow)

time: 275 us -> 291 us (1.058)
  waiting for transfers between devices: 85.6 us -> 98.3 us
    all_gather x1 -> x2, waiting for transfers between devices: 4.72 us -> 17 us  [the longest x1 17 us: local(): left = lax.all_gather(llm_grads[0, :, :half], 'dp', axis=0, tiled=True)]
    dot_general x1 -> x2, matrix products: 7.19 us -> 9.32 us  [the longest x1 5.02 us: local(): jnp.dot(right, w_out[:, half:].T, preferred_element_type=single)]
    unnamed x33 -> x35, local copies, waits for them, and re-layouts: 8.78 us -> 8.12 us
  transfers between devices with their start and end apart: 13 -> 14, of which waited for: 9 -> 9; matrix products, arithmetic and copies ran while one was open for 14% -> 13% of each run, Pallas kernels for 11% -> 11%
where the time goes in v4:
time: 291 us; the launch traced here: 290 us
  waiting for transfers between devices  98.3 us (34%)
  starting transfers between devices  45.9 us (16%)
  matrix products  33.3 us (11%)
  Pallas kernels  30.8 us (11%)
  blocking collectives  26 us (9%)
  local copies, waits for them, and re-layouts  25.6 us (9%)
  other arithmetic  15.1 us (5%)
  between operations  14.8 us (5%)
    ppermute x4, waiting for transfers between devices, from_behind(): return lax.ppermute(block, axis, route)  32.7 us
    all_to_all x1, waiting for transfers between devices, local(): lax.all_to_all(spread, 'cp', split_axis=0, concat_axis=0, tiled=True)  18.5 us
    pallas_call x1, Pallas kernels, backward(): pl.pallas_call(backward_kernel, grid=(groups,), in_specs=own + halo + ids...  18.1 us
    all_gather x1, waiting for transfers between devices, local(): left = lax.all_gather(llm_grads[0, :, :half], 'dp', axis=0, tiled=True)  17 us
    all_gather x1, blocking collectives, local(): whole = lax.all_gather(own_rows, 'dp', axis=0).astype(single)  16.3 us
    all_to_all x1, waiting for transfers between devices, local(): lax.all_to_all(jnp.broadcast_to(own_proj[None], (shards, part, width)), '...  15.1 us
    pallas_call x1, Pallas kernels, attention_calls(): pl.pallas_call(forward_kernel, grid=(groups,), in_specs=own + halo + ids,...  12.7 us
    all_to_all x1, starting transfers between devices, local(): lax.all_to_all(jnp.broadcast_to(own_proj[None], (shards, part, width)), '...  12 us
  transfers between devices with their start and end apart: 14, of which 9 were waited for; matrix products, arithmetic and copies ran while one was open for 13% of the time, Pallas kernels for 11%

profile of v4, /device:TPU:1, one launch (start us, length us, event | category | flops | bytes accessed | tf_op | source)
XLA Modules:
  0.0 289.8 jit_solution(17443009994051712035)
XLA Ops:
  7.2 2.2 fusion.102
  11.9 12.0 %all-to-all-start = ((bf16[32,5,1280]{2,1,0:T(8,128)(2,1)}), bf16[32,5,1280]{2,1,0:T(8,128)(2,1)}, u32[]{:S(2)}, u32[]{:S(2)}) async-start(bf16[32,5,1280]{2,1,0:T(8,128)(2,1)} %broadcast_in_dim.38), calls=%async_computation | async-start | bytes 1310720 | tf_op jit(solution)/shard_map/all_to_all | solution.py:214
  25.2 2.3 slice_bitcast_fusion
  27.5 15.1 %all-to-all-done = bf16[32,5,1280]{2,1,0:T(8,128)(2,1)} async-done(((bf16[32,5,1280]{2,1,0:T(8,128)(2,1)}), bf16[32,5,1280]{2,1,0:T(8,128)(2,1)}, u32[]{:S(2)}, u32[]{:S(2)}) %all-to-all-start) | async-done | bytes 409632 | tf_op jit(solution)/shard_map/all_to_all | solution.py:214
  42.6 2.0 reshape.284
  44.8 9.7 %all-reduce = s32[384]{0:T(512)S(1)} all-reduce(s32[384]{0:T(512)S(1)} %dynamic-update-slice), channel_id=3, replica_groups=mesh['cp'=32,'dp'=8] {'dp'}, use_global_device_ids=true, to_apply=%add | all-reduce | flops 384 | bytes 3072
  55.2 5.0 %fusion.11 = f32[384,320]{0,1:T(8,128)} fusion(bf16[384,4096]{1,0:T(8,128)(2,1)} %bitcast.67, bf16[320,8192]{1,0:T(8,128)(2,1)} %param.17), kind=kOutput, calls=%fused_computation.16 | convolution fusion | flops 1006632960 | bytes 6258688 | tf_op jit(solution)/shard_map/dot_general | solution.py:239
  60.3 17.0 %all-gather.12.cloned.1.call-done = bf16[1,384,4096]{2,1,0:T(8,128)(2,1)} async-done(((bf16[1,48,4096]{2,1,0:T(8,128)(2,1)}), bf16[1,384,4096]{2,1,0:T(8,128)(2,1)}) %all-gather.12.cloned.1.call-update) | async-done | bytes 3145744 | tf_op jit(solution)/shard_map/all_gather | solution.py:209
  77.3 4.3 %fusion.25 = bf16[384,320]{0,1:T(8,128)(2,1)S(1)} fusion(f32[384,320]{0,1:T(8,128)} %fusion.11, bf16[320,8192]{1,0:T(8,128)(2,1)} %param.17, bf16[1,384,4096]{2,1,0:T(8,128)(2,1)} %all-gather.12.cloned.1.call-done), kind=kOutput, calls=%fused_computation.34 | convolution fusion | flops 1006878720 | bytes 6504448 | tf_op jit(solution)/shard_map/dot_general | solution.py:238
  81.6 1.3 convolution_convert_fusion.3
  82.9 9.6 %all-to-all-start.1 = ((bf16[32,24,384]{2,1,0:T(8,128)(2,1)}), bf16[32,24,384]{2,1,0:T(8,128)(2,1)}, u32[]{:S(2)}, u32[]{:S(2)}) async-start(bf16[32,24,384]{2,1,0:T(8,128)(2,1)} %bitcast.64), calls=%async_computation.1 | async-start | bytes 1179648 | tf_op jit(solution)/shard_map/all_to_all | solution.py:247
  92.6 4.1 %collective-permute-start = (bf16[192,2560]{1,0:T(8,128)(2,1)}, bf16[192,2560]{1,0:T(8,128)(2,1)}, u32[]{:S(2)}, u32[]{:S(2)}) collective-permute-start(bf16[192,2560]{1,0:T(8,128)(2,1)} %slice_bitcast_fusion), channel_id=1, source_target_pairs={{0,8},{8,16},{16,24},{24,32},{32,40},{40,48},{48,56},{56,64},{64,7... | collective-permute-start | bytes 2949128 | tf_op jit(solution)/shard_map/ppermute | solution.py:20
  96.7 1.3 collective-permute-start.1
  98.0 23.7 %collective-permute-done.kl_ref.vl_ref = bf16[192,2560]{1,0:T(8,128)(2,1)} collective-permute-done((bf16[192,2560]{1,0:T(8,128)(2,1)}, bf16[192,2560]{1,0:T(8,128)(2,1)}, u32[]{:S(2)}, u32[]{:S(2)}) %collective-permute-start) | collective-permute-done | bytes 983072 | tf_op jit(solution)/shard_map/ppermute | solution.py:20
  121.7 3.2 %collective-permute-done.1.kh_ref.vh_ref = bf16[192,2560]{1,0:T(8,128)(2,1)} collective-permute-done((bf16[192,2560]{1,0:T(8,128)(2,1)}, bf16[192,2560]{1,0:T(8,128)(2,1)}, u32[]{:S(2)}, u32[]{:S(2)}) %collective-permute-start.1) | collective-permute-done | bytes 983072 | tf_op jit(solution)/shard_map/ppermute | solution.py:20
  126.2 1.5 fusion.32
  127.7 1.2 fusion.49
  129.0 2.5 convolution_convert_fusion
  131.5 1.2 collective-permute-start.2
  132.7 3.9 %collective-permute-done.2 = bf16[4,48,5120]{2,1,0:T(8,128)(2,1)} collective-permute-done((bf16[4,48,5120]{2,1,0:T(8,128)(2,1)}, bf16[4,48,5120]{2,1,0:T(8,128)(2,1)}, u32[]{:S(2)}, u32[]{:S(2)}) %collective-permute-start.2) | collective-permute-done | bytes 1966112 | tf_op jit(solution)/shard_map/ppermute | solution.py:31
  136.7 4.1 %add_convert_fusion = bf16[4,48,5120]{2,1,0:T(8,128)(2,1)} fusion(bf16[4,48,5120]{2,1,0:T(8,128)(2,1)} %collective-permute-done.2, bf16[5120,320]{0,1:T(8,128)(2,1)S(1)} %copy-done, bf16[4,2,48,320]{3,2,1,0:T(8,128)(2,1)} %bitcast.63, s32[]{:T(128)S(6)} %select_n.166), kind=kOutput, calls=%fused_computation.3 | convolution fusion | flops 632094720 | bytes 7356420 | tf_op jit(solution)/shard_map/bmh,ih->bmi/dot_general | solution.py:266
  142.2 1.6 reshape.289
  144.2 1.2 fusion.38
  145.5 1.4 copy-done.1
  146.8 12.7 %attention_forward.1 = (bf16[192,1280]{1,0:T(8,128)(2,1)S(1)}, f32[2,192,8]{2,1,0:T(8,128)S(1)}) custom-call(bf16[1,192,3840]{2,1,0:T(8,128)(2,1)S(1)} %copy-done.1, bf16[1,192,3840]{2,1,0:T(8,128)(2,1)S(1)} %copy-done.1, bf16[1,192,3840]{2,1,0:T(8,128)(2,1)S(1)} %copy-done.1, bf16[192,2560]{1,0:T(8,128)(2,1)} %collective-permute-done.kl_ref.vl_ref, ...), custom_call_target="tpu_custom_call" | custom-call | flops 566231040 | bytes 2949120 | tf_op jit(solution)/shard_map/attention_forward/pallas_call | solution.py:161
  160.2 1.5 fusion.31
  161.7 1.5 fusion.30
  163.3 10.2 %reduce-scatter.3.cloned.1.call-done = bf16[1,48,5120]{2,1,0:T(8,128)(2,1)} async-done(((bf16[4,48,5120]{2,1,0:T(8,128)(2,1)}), bf16[1,48,5120]{2,1,0:T(8,128)(2,1)}) %reduce-scatter.3.cloned.1.call-update) | async-done | bytes 491536 | tf_op jit(solution)/shard_map/reduce_scatter | solution.py:38
  173.4 2.1 reshape.290
  175.6 1.6 fusion.37
  177.2 1.5 fusion.35
  179.4 2.8 convolution_convert_fusion.1
  182.9 5.1 %fusion.14.do_ref = bf16[192,1280]{1,0:T(8,128)(2,1)} fusion(s32[1280]{0:T(1024)S(1)} %fusion.69, bf16[192,1280]{1,0:T(8,128)(2,1)} %copy-done.9, bf16[1280,1280]{1,0:T(8,128)(2,1)} %all-gather.8.cloned.1.call-done), kind=kOutput, calls=%fused_computation.20 | convolution fusion | flops 1260421120 | bytes 4264960 | tf_op jit(solution)/shard_map/dot_general | solution.py:319
  188.0 3.5 %add_convert_fusion.1 = bf16[640,1280]{1,0:T(8,128)(2,1)} fusion(bf16[640,1280]{1,0:T(8,128)(2,1)} %collective-permute-done.3, bf16[192,640]{1,0:T(8,128)(2,1)} %fusion.30, bf16[192,1280]{1,0:T(8,128)(2,1)} %copy-done.9), kind=kOutput, calls=%fused_computation.8 | convolution fusion | flops 317030400 | bytes 4014080 | tf_op jit(solution)/shard_map/pi,pj->ij/dot_general | solution.py:306
  194.5 18.1 %attention_backward.1 = (bf16[192,1280]{1,0:T(8,128)(2,1)S(1)}, bf16[2,192,1280]{2,1,0:T(8,128)(2,1)}, f32[2,192,1280]{2,1,0:T(8,128)}, bf16[2,192,1280]{2,1,0:T(8,128)(2,1)}) custom-call(bf16[1,192,3840]{2,1,0:T(8,128)(2,1)} %v_ref.3, bf16[1,192,3840]{2,1,0:T(8,128)(2,1)} %v_ref.3, bf16[1,192,3840]{2,1,0:T(8,128)(2,1)} %v_ref.3, ...), custom_call_target="tpu_custom_call" | custom-call | flops 1415577600 | bytes 2949120 | tf_op jit(solution)/shard_map/attention_backward/pallas_call | solution.py:176
  213.4 1.3 collective-permute-start.5
  214.7 5.0 %collective-permute-start.4 = (bf16[2,192,1280]{2,1,0:T(8,128)(2,1)}, bf16[2,192,1280]{2,1,0:T(8,128)(2,1)}, u32[]{:S(2)}, u32[]{:S(2)}) collective-permute-start(bf16[2,192,1280]{2,1,0:T(8,128)(2,1)} %get-tuple-element.47), channel_id=1, source_target_pairs={{0,8},{8,16},{16,24},{24,32},{32,40},{40,48},{48,56},{56,64},{64,7... | collective-permute-start | bytes 2949128 | tf_op jit(solution)/shard_map/ppermute | solution.py:20
  219.8 2.0 reshape.291
  221.8 2.3 pad_maximum_fusion
  224.1 10.5 %all-to-all-start.2 = ((bf16[32,8,1280]{2,1,0:T(8,128)(2,1)}), bf16[32,8,1280]{2,1,0:T(8,128)(2,1)}, u32[]{:S(2)}, u32[]{:S(2)}) async-start(bf16[32,8,1280]{2,1,0:T(8,128)(2,1)} %pad_maximum_fusion), calls=%async_computation.4 | async-start | bytes 1310720 | tf_op jit(solution)/shard_map/all_to_all | solution.py:333
  234.6 4.6 %collective-permute-done.5 = bf16[2,192,1280]{2,1,0:T(8,128)(2,1)} collective-permute-done((bf16[2,192,1280]{2,1,0:T(8,128)(2,1)}, bf16[2,192,1280]{2,1,0:T(8,128)(2,1)}, u32[]{:S(2)}, u32[]{:S(2)}) %collective-permute-start.5) | collective-permute-done | bytes 983072 | tf_op jit(solution)/shard_map/ppermute | solution.py:20
  239.2 1.2 collective-permute-done.4
  240.4 2.4 add_convert_fusion.2
  242.9 1.2 maximum_bitcast_fusion
  244.1 18.5 %all-to-all-done.2 = bf16[32,8,1280]{2,1,0:T(8,128)(2,1)} async-done(((bf16[32,8,1280]{2,1,0:T(8,128)(2,1)}), bf16[32,8,1280]{2,1,0:T(8,128)(2,1)}, u32[]{:S(2)}, u32[]{:S(2)}) %all-to-all-start.2) | async-done | bytes 655392 | tf_op jit(solution)/shard_map/all_to_all | solution.py:333
  262.6 1.2 convert_reduce_fusion
  263.9 16.3 %all-gather.3 = bf16[64,1280]{1,0:T(8,128)(2,1)S(1)} all-gather(bf16[8,1280]{1,0:T(8,128)(2,1)S(1)} %pad_maximum_fusion.1), channel_id=5, replica_groups=mesh['cp'=32,'dp'=8] {'dp'}, dimensions={0}, use_global_device_ids=true | all-gather | bytes 184320 | tf_op jit(solution)/shard_map/all_gather | solution.py:340
  281.6 1.7 reshape.292
  (86 shorter events, 14.7 us)
Async XLA Ops:
  7.2 121.8 %copy-start = (bf16[5120,320]{0,1:T(8,128)(2,1)S(1)}, bf16[5120,320]{0,1:T(8,128)(2,1)}, u32[]{:S(2)}) copy-start(bf16[5120,320]{0,1:T(8,128)(2,1)} %param.16) | copy-start | bytes 9830404
  7.2 16.8 %copy-start.15 = (u32[256]{0:T(256)S(1)}, u32[256]{0:T(256)}, u32[]{:S(2)}) copy-start(u32[256]{0:T(256)} %constant.178) | copy-start | bytes 3076
  7.2 47.4 %all-gather.10.cloned.1.call-start = ((), (), s32[]{:S(2)}) async-start(), calls=%async_computation.8 | async-start | bytes 3538944 | tf_op jit(solution)/shard_map/all_gather | solution.py:210
  9.4 35.2 %copy-start.14 = (s32[1,48]{1,0:T(1,128)S(1)}, s32[1,48]{1,0:T(1,128)}, u32[]{:S(2)}) copy-start(s32[1,48]{1,0:T(1,128)} %param.11) | copy-start | bytes 580
  9.5 67.8 %all-gather.12.cloned.1.call-start = ((), (), s32[]{:S(2)}) async-start(), calls=%async_computation.9 | async-start | bytes 3538944 | tf_op jit(solution)/shard_map/all_gather | solution.py:209
  11.9 30.7 %all-to-all-start = ((bf16[32,5,1280]{2,1,0:T(8,128)(2,1)}), bf16[32,5,1280]{2,1,0:T(8,128)(2,1)}, u32[]{:S(2)}, u32[]{:S(2)}) async-start(bf16[32,5,1280]{2,1,0:T(8,128)(2,1)} %broadcast_in_dim.38), calls=%async_computation | async-start | bytes 1310720 | tf_op jit(solution)/shard_map/all_to_all | solution.py:214
  23.9 101.1 %all-gather.8.cloned.1.call-start = ((), (), s32[]{:S(2)}) async-start(), calls=%async_computation.5 | async-start | bytes 3686400 | tf_op jit(solution)/shard_map/all_gather | solution.py:226
  82.9 42.0 %all-to-all-start.1 = ((bf16[32,24,384]{2,1,0:T(8,128)(2,1)}), bf16[32,24,384]{2,1,0:T(8,128)(2,1)}, u32[]{:S(2)}, u32[]{:S(2)}) async-start(bf16[32,24,384]{2,1,0:T(8,128)(2,1)} %bitcast.64), calls=%async_computation.1 | async-start | bytes 1179648 | tf_op jit(solution)/shard_map/all_to_all | solution.py:247
  92.6 80.9 %reduce-scatter.3.cloned.1.call-start = ((), (), s32[]{:S(2)}) async-start(), calls=%async_computation.6 | async-start | bytes 2457600 | tf_op jit(solution)/shard_map/reduce_scatter | solution.py:38
  92.6 29.1 %collective-permute-start = (bf16[192,2560]{1,0:T(8,128)(2,1)}, bf16[192,2560]{1,0:T(8,128)(2,1)}, u32[]{:S(2)}, u32[]{:S(2)}) collective-permute-start(bf16[192,2560]{1,0:T(8,128)(2,1)} %slice_bitcast_fusion), channel_id=1, source_target_pairs={{0,8},{8,16},{16,24},{24,32},{32,40},{40,48},{48,56},{56,64},{64,7... | collective-permute-start | bytes 2949128 | tf_op jit(solution)/shard_map/ppermute | solution.py:20
  96.7 28.3 %collective-permute-start.1 = (bf16[192,2560]{1,0:T(8,128)(2,1)}, bf16[192,2560]{1,0:T(8,128)(2,1)}, u32[]{:S(2)}, u32[]{:S(2)}) collective-permute-start(bf16[192,2560]{1,0:T(8,128)(2,1)} %slice_bitcast_fusion), channel_id=1, source_target_pairs={{8,0},{16,8},{24,16},{32,24},{40,32},{48,40},{56,48},{64,56},{72,6... | collective-permute-start | bytes 2949128 | tf_op jit(solution)/shard_map/ppermute | solution.py:20
  129.0 2.5 copy-start.11
  131.5 5.2 %collective-permute-start.2 = (bf16[4,48,5120]{2,1,0:T(8,128)(2,1)}, bf16[4,48,5120]{2,1,0:T(8,128)(2,1)}, u32[]{:S(2)}, u32[]{:S(2)}) collective-permute-start(bf16[4,48,5120]{2,1,0:T(8,128)(2,1)} %convolution_convert_fusion), channel_id=1, source_target_pairs={{0,1},{1,0},{2,3},{3,2},{4,5},{5,4},{6,7},{7,6},{8,9},{9,8},{10,11... | collective-permute-start | bytes 5898248 | tf_op jit(solution)/shard_map/ppermute | solution.py:31
  132.7 8.3 %copy-start.13 = (s32[1,1536]{1,0:T(1,128)S(1)}, s32[1,1536]{1,0:T(1,128)}, u32[]{:S(2)}) copy-start(s32[1,1536]{1,0:T(1,128)} %param.12) | copy-start | bytes 18436
  140.8 78.9 %reduce-scatter.5.cloned.1.call-start = ((), (), s32[]{:S(2)}) async-start(), calls=%async_computation.7 | async-start | bytes 2048000 | tf_op jit(solution)/shard_map/reduce_scatter | solution.py:38
  145.5 1.4 copy-start.1
  159.5 0.7 copy-start.7
  160.2 1.5 copy-start.4
  160.2 15.4 %copy-start.12 = (f32[1280]{0:T(1024)S(1)}, f32[1280]{0:T(1024)}, u32[]{:S(2)}) copy-start(f32[1280]{0:T(1024)} %param.14) | copy-start | bytes 15364
  178.7 0.8 copy-start.9
  182.2 5.7 %collective-permute-start.3 = (bf16[640,1280]{1,0:T(8,128)(2,1)}, bf16[640,1280]{1,0:T(8,128)(2,1)}, u32[]{:S(2)}, u32[]{:S(2)}) collective-permute-start(bf16[640,1280]{1,0:T(8,128)(2,1)} %convolution_convert_fusion.1), channel_id=1, source_target_pairs={{0,1},{1,0},{2,3},{3,2},{4,5},{5,4},{6,7},{7,6},{8,9},{9,8},{10,11... | collective-permute-start | bytes 4915208 | tf_op jit(solution)/shard_map/ppermute | solution.py:31
  191.5 1.0 copy-start.5
  192.6 1.0 copy-start.6
  193.6 0.9 copy-start.8
  212.6 0.8 copy-start.2
  213.4 25.8 %collective-permute-start.5 = (bf16[2,192,1280]{2,1,0:T(8,128)(2,1)}, bf16[2,192,1280]{2,1,0:T(8,128)(2,1)}, u32[]{:S(2)}, u32[]{:S(2)}) collective-permute-start(bf16[2,192,1280]{2,1,0:T(8,128)(2,1)} %get-tuple-element.48), channel_id=1, source_target_pairs={{8,0},{16,8},{24,16},{32,24},{40,32},{48,40},{56,48},{64,56},{72,6... | collective-permute-start | bytes 2949128 | tf_op jit(solution)/shard_map/ppermute | solution.py:20
  214.7 25.7 %collective-permute-start.4 = (bf16[2,192,1280]{2,1,0:T(8,128)(2,1)}, bf16[2,192,1280]{2,1,0:T(8,128)(2,1)}, u32[]{:S(2)}, u32[]{:S(2)}) collective-permute-start(bf16[2,192,1280]{2,1,0:T(8,128)(2,1)} %get-tuple-element.47), channel_id=1, source_target_pairs={{0,8},{8,16},{16,24},{24,32},{32,40},{40,48},{48,56},{56,64},{64,7... | collective-permute-start | bytes 2949128 | tf_op jit(solution)/shard_map/ppermute | solution.py:20
  224.1 38.5 %all-to-all-start.2 = ((bf16[32,8,1280]{2,1,0:T(8,128)(2,1)}), bf16[32,8,1280]{2,1,0:T(8,128)(2,1)}, u32[]{:S(2)}, u32[]{:S(2)}) async-start(bf16[32,8,1280]{2,1,0:T(8,128)(2,1)} %pad_maximum_fusion), calls=%async_computation.4 | async-start | bytes 1310720 | tf_op jit(solution)/shard_map/all_to_all | solution.py:333
  240.4 2.5 copy-start.3
  280.3 0.7 copy-start.10
Sparse Core Ops, SparseCore 0:
  10.4 34.5 all-gather.9
  46.9 30.3 all-gather.11
  79.1 30.9 all-gather.7
  140.9 32.4 reduce-scatter.2
  191.7 27.4 reduce-scatter.4

commit v5 on v3

--- a/solution.py
+++ b/solution.py
@@ -25,11 +25,8 @@
     return lax.dynamic_index_in_dim(block, core if own else 1 - core, dim, keepdims=False)
 
 
-def added_on_chip(partial_of):
-    count = lax.axis_size("dp")
-    swap = [(i, i ^ 1) for i in range(count)]
-    received = lax.ppermute(partial_of(False).astype(jnp.bfloat16), "dp", swap)
-    return (partial_of(True) + received.astype(jnp.float32)).astype(jnp.bfloat16)
+def from_sibling(block):
+    return lax.ppermute(block, "dp", [(i, i ^ 1) for i in range(lax.axis_size("dp"))])
 
 
 def scattered_over_y(pair):
@@ -220,7 +217,10 @@
         (proj_parts, qkv[0, :, width:], llm_owner[0])
     )
     owners = lax.all_gather(own_owners, "dp", axis=0)
-    gathered, proj_parts, owners = lax.optimization_barrier((gathered, proj_parts, owners))
+    chip_in = jnp.concatenate([w_in, from_sibling(w_in)], axis=1)
+    gathered, proj_parts, owners, chip_in = lax.optimization_barrier(
+        (gathered, proj_parts, owners, chip_in)
+    )
     full_proj = lax.all_gather(proj_parts, "dp", axis=0, tiled=True)
     low = from_behind(key_values, "cp", 1)
     high = from_behind(key_values, "cp", -1)
@@ -257,16 +257,12 @@
     )
     saved_pre = pre_act.astype(single)
     d_pre = (d_hidden * gelu_slope(saved_pre)).astype(narrow)
-    d_norm = added_on_chip(
-        lambda own: (
-            jnp.einsum(
-                "bmh,ih->bmi",
-                by_core(d_pre.reshape(batches // 2, 2, row_count, hidden), 1, own),
-                w_in,
-                preferred_element_type=single,
-            )
-        )
-    )
+    halves = d_pre.reshape(batches // 2, 2, row_count, hidden)
+    chip_pre = jnp.concatenate(
+        [by_core(halves, 1, True), from_sibling(by_core(halves, 1, False))], axis=2
+    )
+    d_norm = jnp.einsum("bmh,ih->bmi", chip_pre, chip_in, preferred_element_type=single)
+    d_norm = d_norm.astype(narrow)
     d_norm = scattered_over_y(d_norm)
     segment = jnp.repeat(image_ids[0], 4)
     seg_rim = jnp.full((patches,), -1, jnp.int32)
@@ -284,13 +280,11 @@
         pick_columns = (feature == column_base + core * part).astype(narrow)
         return jnp.dot(attention, pick_columns, preferred_element_type=single).astype(narrow)
 
-    other_features, own_features = features_of(1 - core), features_of(core)
+    features = jnp.concatenate([features_of(core), from_sibling(features_of(1 - core))], axis=0)
     stream_wide = stream[0].astype(single)
     inverse = lax.rsqrt(jnp.mean(stream_wide * stream_wide, axis=-1, keepdims=True) + EPS)
     normed = stream_wide * inverse
-    d_norm, other_features, own_features = lax.optimization_barrier(
-        (d_norm, other_features, own_features)
-    )
+    d_norm, features = lax.optimization_barrier((d_norm, features))
     d_norm = lax.optimization_barrier(d_norm.reshape(patches, width)).astype(single)
     gain_part = jnp.sum(d_norm * normed, axis=0)
     d_normed = d_norm * ln_gain
@@ -298,14 +292,10 @@
         inverse * (d_normed - normed * jnp.mean(d_normed * normed, axis=-1, keepdims=True))
     ).astype(narrow)
     d_stream = lax.optimization_barrier(d_stream)
-    d_proj_pair = added_on_chip(
-        lambda own: jnp.einsum(
-            "pi,pj->ij",
-            own_features if own else other_features,
-            d_stream,
-            preferred_element_type=single,
-        )
-    )
+    chip_stream = jnp.concatenate([d_stream, from_sibling(d_stream)], axis=0)
+    d_proj_pair = jnp.einsum(
+        "pi,pj->ij", features, chip_stream, preferred_element_type=single
+    ).astype(narrow)
     d_out = jnp.einsum(
         "pj,ij->pi", d_stream, full_proj, preferred_element_type=single
     ).astype(narrow)

time: 275 us -> 259 us (0.942)
  the two profiles are of different devices: /device:TPU:1 before, /device:TPU:35 now
where the time goes in v5:
time: 259 us; the launch traced here: 258 us
  waiting for transfers between devices  84.2 us (33%)
  starting transfers between devices  43.5 us (17%)
  Pallas kernels  29.4 us (11%)
  matrix products  26.2 us (10%)
  blocking collectives  23.8 us (9%)
  other arithmetic  19.1 us (7%)
  local copies, waits for them, and re-layouts  17 us (7%)
  between operations  14.9 us (6%)
    ppermute x4, waiting for transfers between devices, from_behind(): return lax.ppermute(block, axis, route)  37.2 us
    pallas_call x1, Pallas kernels, backward(): pl.pallas_call(backward_kernel, grid=(groups,), in_specs=own + halo + ids...  17.7 us
    all_to_all x1, waiting for transfers between devices, local(): lax.all_to_all(spread, 'cp', split_axis=0, concat_axis=0, tiled=True)  17.5 us
    all_to_all x1, waiting for transfers between devices, local(): lax.all_to_all(jnp.broadcast_to(own_proj[None], (shards, part, width)), '...  15.7 us
    all_gather x1, blocking collectives, local(): whole = lax.all_gather(own_rows, 'dp', axis=0).astype(single)  14.7 us
    pallas_call x1, Pallas kernels, attention_calls(): pl.pallas_call(forward_kernel, grid=(groups,), in_specs=own + halo + ids,...  11.7 us
    ppermute x4, starting transfers between devices, from_behind(): return lax.ppermute(block, axis, route)  10.7 us
    reduce_scatter x2, waiting for transfers between devices, scattered_over_y(): lax.psum_scatter(pair, 'dp', scatter_dimension=0, axis_index_groups=group...  10.6 us
  transfers between devices with their start and end apart: 15, of which 11 were waited for; matrix products, arithmetic and copies ran while one was open for 16% of the time, Pallas kernels for 11%

profile of v5, /device:TPU:35, one launch (start us, length us, event | category | flops | bytes accessed | tf_op | source)
XLA Modules:
  0.0 258.2 jit_solution(3204767383289189351)
XLA Ops:
  8.7 0.9 broadcast_in_dim.38
  9.6 10.6 %all-to-all-start = ((bf16[32,5,1280]{2,1,0:T(8,128)(2,1)}), bf16[32,5,1280]{2,1,0:T(8,128)(2,1)S(1)}, u32[]{:S(2)}, u32[]{:S(2)}) async-start(bf16[32,5,1280]{2,1,0:T(8,128)(2,1)} %broadcast_in_dim.38), calls=%async_computation | async-start | bytes 1310720 | tf_op jit(solution)/shard_map/all_to_all | solution.py:209
  20.3 1.3 dynamic-slice
  22.2 1.0 slice_bitcast_fusion
  23.2 15.7 %all-to-all-done = bf16[32,5,1280]{2,1,0:T(8,128)(2,1)S(1)} async-done(((bf16[32,5,1280]{2,1,0:T(8,128)(2,1)}), bf16[32,5,1280]{2,1,0:T(8,128)(2,1)S(1)}, u32[]{:S(2)}, u32[]{:S(2)}) %all-to-all-start) | async-done | bytes 409632 | tf_op jit(solution)/shard_map/all_to_all | solution.py:209
  38.9 0.9 reshape.283
  40.0 9.1 %all-reduce = s32[384]{0:T(512)S(1)} all-reduce(s32[384]{0:T(512)S(1)} %dynamic-update-slice), channel_id=3, replica_groups=mesh['cp'=32,'dp'=8] {'dp'}, use_global_device_ids=true, to_apply=%add | all-reduce | flops 384 | bytes 3072
  49.2 6.1 %pad_maximum_fusion = bf16[5120,640]{0,1:T(8,128)(2,1)} fusion(bf16[5120,320]{0,1:T(8,128)(2,1)} %collective-permute-done, bf16[5120,320]{0,1:T(8,128)(2,1)} %param.16), kind=kLoop, calls=%fused_computation | loop fusion | flops 13107200 | bytes 13107200 | tf_op jit(solution)/shard_map/concatenate | solution.py:220
  55.4 1.1 all-gather.8.cloned.1.call-done
  57.1 7.2 %convolution_convert_fusion.3 = bf16[384,320]{0,1:T(8,128)(2,1)S(1)} fusion(bf16[384,8192]{1,0:T(8,128)(2,1)} %bitcast.51, bf16[320,8192]{1,0:T(8,128)(2,1)} %param.17), kind=kOutput, calls=%fused_computation.28 | convolution fusion | flops 2013388800 | bytes 11780096 | tf_op jit(solution)/shard_map/dot_general | solution.py:236
  64.3 1.3 convolution_convert_fusion.2
  65.7 9.5 %all-to-all-start.1 = ((bf16[32,24,384]{2,1,0:T(8,128)(2,1)}), bf16[32,24,384]{2,1,0:T(8,128)(2,1)}, u32[]{:S(2)}, u32[]{:S(2)}) async-start(bf16[32,24,384]{2,1,0:T(8,128)(2,1)} %bitcast.5), calls=%async_computation.1 | async-start | bytes 1179648 | tf_op jit(solution)/shard_map/all_to_all | solution.py:243
  75.3 3.1 %collective-permute-start.1 = (bf16[192,2560]{1,0:T(8,128)(2,1)}, bf16[192,2560]{1,0:T(8,128)(2,1)S(1)}, u32[]{:S(2)}, u32[]{:S(2)}) collective-permute-start(bf16[192,2560]{1,0:T(8,128)(2,1)} %slice_bitcast_fusion), channel_id=1, source_target_pairs={{0,8},{8,16},{16,24},{24,32},{32,40},{40,48},{48,56},{56,64},{64,7... | collective-permute-start | bytes 2949128 | tf_op jit(solution)/shard_map/ppermute | solution.py:20
  78.4 2.2 collective-permute-start.2
  80.6 24.0 %collective-permute-done.1.kl_ref.vl_ref = bf16[192,2560]{1,0:T(8,128)(2,1)S(1)} collective-permute-done((bf16[192,2560]{1,0:T(8,128)(2,1)}, bf16[192,2560]{1,0:T(8,128)(2,1)S(1)}, u32[]{:S(2)}, u32[]{:S(2)}) %collective-permute-start.1) | collective-permute-done | bytes 983072 | tf_op jit(solution)/shard_map/ppermute | solution.py:20
  104.6 2.9 %collective-permute-done.2.kh_ref.vh_ref = bf16[192,2560]{1,0:T(8,128)(2,1)S(1)} collective-permute-done((bf16[192,2560]{1,0:T(8,128)(2,1)}, bf16[192,2560]{1,0:T(8,128)(2,1)S(1)}, u32[]{:S(2)}, u32[]{:S(2)}) %collective-permute-start.2) | collective-permute-done | bytes 983072 | tf_op jit(solution)/shard_map/ppermute | solution.py:20
  107.5 1.2 convert_reduce_fusion.1
  108.7 1.5 fusion.17
  110.3 1.2 fusion.37
  111.5 1.1 collective-permute-start.3
  112.6 1.0 collective-permute-done.3
  113.6 5.9 %fusion.3 = bf16[4,48,5120]{2,1,0:T(8,128)(2,1)} fusion(bf16[5120,640]{0,1:T(8,128)(2,1)} %pad_maximum_fusion, bf16[4,48,320]{2,1,0:T(8,128)(2,1)S(1)} %collective-permute-done.3, bf16[4,48,320]{2,1,0:T(8,128)(2,1)S(1)} %get-tuple-element.54), kind=kOutput, calls=%fused_computation.5 | convolution fusion | flops 1259765760 | bytes 8765440 | tf_op jit(solution)/shard_map/bmh,ih->bmi/dot_general | solution.py:264
  120.5 1.1 broadcast_in_dim.42
  121.7 2.2 reshape.288
  125.4 1.4 concatenate.30
  127.6 1.2 fusion.23
  129.4 0.9 copy-done.2
  130.3 11.7 %attention_forward.1 = (bf16[192,1280]{1,0:T(8,128)(2,1)S(1)}, f32[2,192,8]{2,1,0:T(8,128)S(1)}) custom-call(bf16[1,192,3840]{2,1,0:T(8,128)(2,1)S(1)} %copy-done.1, bf16[1,192,3840]{2,1,0:T(8,128)(2,1)S(1)} %copy-done.1, bf16[1,192,3840]{2,1,0:T(8,128)(2,1)S(1)} %copy-done.1, bf16[192,2560]{1,0:T(8,128)(2,1)S(1)} %collective-permute-done.1.kl_ref.vl_ref, ...), custom_call_target="tpu_custom_call" | custom-call | flops 566231040 | bytes 2949120 | tf_op jit(solution)/shard_map/attention_forward/pallas_call | solution.py:158
  144.5 0.9 pad_maximum_fusion.2
  145.3 7.4 %reduce-scatter.3.cloned.1.call-done = bf16[1,48,5120]{2,1,0:T(8,128)(2,1)} async-done(((bf16[4,48,5120]{2,1,0:T(8,128)(2,1)}), bf16[1,48,5120]{2,1,0:T(8,128)(2,1)}) %reduce-scatter.3.cloned.1.call-update) | async-done | bytes 491536 | tf_op jit(solution)/shard_map/reduce_scatter | solution.py:35
  152.7 1.3 reshape.289
  154.5 1.1 fusion.20
  156.2 5.1 %fusion.9.do_ref = bf16[192,1280]{1,0:T(8,128)(2,1)} fusion(s32[1280]{0:T(1024)S(1)} %fusion.56, bf16[192,1280]{1,0:T(8,128)(2,1)} %fusion.20, bf16[1280,1280]{1,0:T(8,128)(2,1)} %all-gather.6.cloned.1.call-done), kind=kOutput, calls=%fused_computation.13 | convolution fusion | flops 1260421120 | bytes 4264960 | tf_op jit(solution)/shard_map/dot_general | solution.py:305
  161.4 3.5 %convolution_convert_fusion = bf16[640,1280]{1,0:T(8,128)(2,1)} fusion(bf16[384,640]{1,0:T(8,128)(2,1)S(1)} %copy-done.11, bf16[192,1280]{1,0:T(8,128)(2,1)} %collective-permute-done.5, bf16[192,1280]{1,0:T(8,128)(2,1)} %fusion.20), kind=kOutput, calls=%fused_computation.11 | convolution fusion | flops 631930880 | bytes 3112960 | tf_op jit(solution)/shard_map/pi,pj->ij/dot_general | solution.py:296
  164.9 1.0 copy-done.6
  165.9 17.7 %attention_backward.1 = (bf16[192,1280]{1,0:T(8,128)(2,1)S(1)}, bf16[2,192,1280]{2,1,0:T(8,128)(2,1)}, f32[2,192,1280]{2,1,0:T(8,128)}, bf16[2,192,1280]{2,1,0:T(8,128)(2,1)}) custom-call(bf16[1,192,3840]{2,1,0:T(8,128)(2,1)} %v_ref.3, bf16[1,192,3840]{2,1,0:T(8,128)(2,1)} %v_ref.3, bf16[1,192,3840]{2,1,0:T(8,128)(2,1)} %v_ref.3, ...), custom_call_target="tpu_custom_call" | custom-call | flops 1415577600 | bytes 2949120 | tf_op jit(solution)/shard_map/attention_backward/pallas_call | solution.py:173
  183.7 3.2 %collective-permute-start.6 = (bf16[2,192,1280]{2,1,0:T(8,128)(2,1)}, bf16[2,192,1280]{2,1,0:T(8,128)(2,1)}, u32[]{:S(2)}, u32[]{:S(2)}) collective-permute-start(bf16[2,192,1280]{2,1,0:T(8,128)(2,1)} %get-tuple-element.47), channel_id=1, source_target_pairs={{0,8},{8,16},{16,24},{24,32},{32,40},{40,48},{48,56},{56,64},{64,7... | collective-permute-start | bytes 2949128 | tf_op jit(solution)/shard_map/ppermute | solution.py:20
  186.9 2.2 collective-permute-start.7
  189.2 3.3 %reduce-scatter.5.cloned.1.call-done = bf16[160,1280]{1,0:T(8,128)(2,1)} async-done(((bf16[640,1280]{1,0:T(8,128)(2,1)}), bf16[160,1280]{1,0:T(8,128)(2,1)}) %reduce-scatter.5.cloned.1.call-update) | async-done | bytes 409616 | tf_op jit(solution)/shard_map/reduce_scatter | solution.py:35
  192.4 1.2 reshape.290
  193.7 1.2 pad_maximum_fusion.1
  194.9 9.5 %all-to-all-start.2 = ((bf16[32,8,1280]{2,1,0:T(8,128)(2,1)}), bf16[32,8,1280]{2,1,0:T(8,128)(2,1)S(1)}, u32[]{:S(2)}, u32[]{:S(2)}) async-start(bf16[32,8,1280]{2,1,0:T(8,128)(2,1)} %pad_maximum_fusion.1), calls=%async_computation.4 | async-start | bytes 1310720 | tf_op jit(solution)/shard_map/all_to_all | solution.py:319
  204.4 5.9 %collective-permute-done.6 = bf16[2,192,1280]{2,1,0:T(8,128)(2,1)} collective-permute-done((bf16[2,192,1280]{2,1,0:T(8,128)(2,1)}, bf16[2,192,1280]{2,1,0:T(8,128)(2,1)}, u32[]{:S(2)}, u32[]{:S(2)}) %collective-permute-start.6) | collective-permute-done | bytes 983072 | tf_op jit(solution)/shard_map/ppermute | solution.py:20
  210.3 4.4 %collective-permute-done.7 = bf16[2,192,1280]{2,1,0:T(8,128)(2,1)} collective-permute-done((bf16[2,192,1280]{2,1,0:T(8,128)(2,1)}, bf16[2,192,1280]{2,1,0:T(8,128)(2,1)}, u32[]{:S(2)}, u32[]{:S(2)}) %collective-permute-start.7) | collective-permute-done | bytes 983072 | tf_op jit(solution)/shard_map/ppermute | solution.py:20
  214.7 1.9 add_convert_fusion
  216.6 1.2 maximum_bitcast_fusion
  217.8 17.5 %all-to-all-done.2 = bf16[32,8,1280]{2,1,0:T(8,128)(2,1)S(1)} async-done(((bf16[32,8,1280]{2,1,0:T(8,128)(2,1)}), bf16[32,8,1280]{2,1,0:T(8,128)(2,1)S(1)}, u32[]{:S(2)}, u32[]{:S(2)}) %all-to-all-start.2) | async-done | bytes 655392 | tf_op jit(solution)/shard_map/all_to_all | solution.py:319
  235.5 14.7 %all-gather.2 = bf16[64,1280]{1,0:T(8,128)(2,1)S(1)} all-gather(bf16[8,1280]{1,0:T(8,128)(2,1)S(1)} %pad_maximum_fusion.3), channel_id=4, replica_groups=mesh['cp'=32,'dp'=8] {'dp'}, dimensions={0}, use_global_device_ids=true | all-gather | bytes 184320 | tf_op jit(solution)/shard_map/all_gather | solution.py:326
  (84 shorter events, 11.7 us)
Async XLA Ops:
  7.2 1.5 copy-start
  7.2 15.0 %copy-start.1 = (bf16[1,192,3840]{2,1,0:T(8,128)(2,1)S(1)}, bf16[1,192,3840]{2,1,0:T(8,128)(2,1)}, u32[]{:S(2)}) copy-start(bf16[1,192,3840]{2,1,0:T(8,128)(2,1)} %v_ref.3) | copy-start | bytes 4423684
  7.2 32.7 %copy-start.14 = (s32[1,48]{1,0:T(1,128)S(1)}, s32[1,48]{1,0:T(1,128)}, u32[]{:S(2)}) copy-start(s32[1,48]{1,0:T(1,128)} %param.11) | copy-start | bytes 580
  7.2 49.3 %all-gather.8.cloned.1.call-start = ((), (), s32[]{:S(2)}) async-start(), calls=%async_computation.8 | async-start | bytes 7077888 | tf_op jit(solution)/shard_map/all_gather | solution.py:205
  7.9 41.3 %collective-permute-start = (bf16[5120,320]{0,1:T(8,128)(2,1)}, bf16[5120,320]{0,1:T(8,128)(2,1)}, u32[]{:S(2)}, u32[]{:S(2)}) collective-permute-start(bf16[5120,320]{0,1:T(8,128)(2,1)} %param.16), channel_id=1, source_target_pairs={{0,1},{1,0},{2,3},{3,2},{4,5},{5,4},{6,7},{7,6},{8,9},{9,8},{10,11... | collective-permute-start | bytes 9830408 | tf_op jit(solution)/shard_map/ppermute | solution.py:29
  9.6 29.3 %all-to-all-start = ((bf16[32,5,1280]{2,1,0:T(8,128)(2,1)}), bf16[32,5,1280]{2,1,0:T(8,128)(2,1)S(1)}, u32[]{:S(2)}, u32[]{:S(2)}) async-start(bf16[32,5,1280]{2,1,0:T(8,128)(2,1)} %broadcast_in_dim.38), calls=%async_computation | async-start | bytes 1310720 | tf_op jit(solution)/shard_map/all_to_all | solution.py:209
  20.2 87.3 %all-gather.6.cloned.1.call-start = ((), (), s32[]{:S(2)}) async-start(), calls=%async_computation.5 | async-start | bytes 3686400 | tf_op jit(solution)/shard_map/all_gather | solution.py:224
  65.7 41.8 %all-to-all-start.1 = ((bf16[32,24,384]{2,1,0:T(8,128)(2,1)}), bf16[32,24,384]{2,1,0:T(8,128)(2,1)}, u32[]{:S(2)}, u32[]{:S(2)}) async-start(bf16[32,24,384]{2,1,0:T(8,128)(2,1)} %bitcast.5), calls=%async_computation.1 | async-start | bytes 1179648 | tf_op jit(solution)/shard_map/all_to_all | solution.py:243
  75.2 77.5 %reduce-scatter.3.cloned.1.call-start = ((), (), s32[]{:S(2)}) async-start(), calls=%async_computation.6 | async-start | bytes 2457600 | tf_op jit(solution)/shard_map/reduce_scatter | solution.py:35
  75.3 29.3 %collective-permute-start.1 = (bf16[192,2560]{1,0:T(8,128)(2,1)}, bf16[192,2560]{1,0:T(8,128)(2,1)S(1)}, u32[]{:S(2)}, u32[]{:S(2)}) collective-permute-start(bf16[192,2560]{1,0:T(8,128)(2,1)} %slice_bitcast_fusion), channel_id=1, source_target_pairs={{0,8},{8,16},{16,24},{24,32},{32,40},{40,48},{48,56},{56,64},{64,7... | collective-permute-start | bytes 2949128 | tf_op jit(solution)/shard_map/ppermute | solution.py:20
  78.4 29.1 %collective-permute-start.2 = (bf16[192,2560]{1,0:T(8,128)(2,1)}, bf16[192,2560]{1,0:T(8,128)(2,1)S(1)}, u32[]{:S(2)}, u32[]{:S(2)}) collective-permute-start(bf16[192,2560]{1,0:T(8,128)(2,1)} %slice_bitcast_fusion), channel_id=1, source_target_pairs={{8,0},{16,8},{24,16},{32,24},{40,32},{48,40},{56,48},{64,56},{72,6... | collective-permute-start | bytes 2949128 | tf_op jit(solution)/shard_map/ppermute | solution.py:20
  111.5 2.1 collective-permute-start.3
  119.6 72.8 %reduce-scatter.5.cloned.1.call-start = ((), (), s32[]{:S(2)}) async-start(), calls=%async_computation.7 | async-start | bytes 2048000 | tf_op jit(solution)/shard_map/reduce_scatter | solution.py:35
  129.4 0.9 copy-start.2
  142.0 1.3 copy-start.4
  142.0 2.2 copy-start.7
  142.0 12.0 %copy-start.9 = (bf16[1,192,1280]{2,1,0:T(8,128)(2,1)S(1)}, bf16[1,192,1280]{2,1,0:T(8,128)(2,1)}, u32[]{:S(2)}) copy-start(bf16[1,192,1280]{2,1,0:T(8,128)(2,1)} %param.13) | copy-start | bytes 1474564
  142.0 12.0 %copy-start.12 = (f32[1280]{0:T(1024)S(1)}, f32[1280]{0:T(1024)}, u32[]{:S(2)}) copy-start(f32[1280]{0:T(1024)} %param.14) | copy-start | bytes 15364
  142.0 12.0 %copy-start.13 = (f32[192]{0:T(256)S(1)}, f32[192]{0:T(256)}, u32[]{:S(2)}) copy-start(f32[192]{0:T(256)} %add_rsqrt_fusion) | copy-start | bytes 2308
  142.9 1.6 collective-permute-start.4
  155.6 5.8 %collective-permute-start.5 = (bf16[192,1280]{1,0:T(8,128)(2,1)}, bf16[192,1280]{1,0:T(8,128)(2,1)}, u32[]{:S(2)}, u32[]{:S(2)}) collective-permute-start(bf16[192,1280]{1,0:T(8,128)(2,1)} %fusion.20), channel_id=1, source_target_pairs={{0,1},{1,0},{2,3},{3,2},{4,5},{5,4},{6,7},{7,6},{8,9},{9,8},{10,11... | collective-permute-start | bytes 1474568 | tf_op jit(solution)/shard_map/ppermute | solution.py:29
  156.2 5.2 %copy-start.11 = (bf16[384,640]{1,0:T(8,128)(2,1)S(1)}, bf16[384,640]{1,0:T(8,128)(2,1)}, u32[]{:S(2)}) copy-start(bf16[384,640]{1,0:T(8,128)(2,1)} %pad_maximum_fusion.2) | copy-start | bytes 1474564
  161.4 3.5 %copy-start.3 = (s32[192,1]{1,0:T(8,128)S(1)}, s32[192,1]{1,0:T(8,128)}, u32[]{:S(2)}) copy-start(s32[192,1]{1,0:T(8,128)} %copy.35.rows_ref) | copy-start | bytes 2308
  161.4 3.5 %copy-start.5 = (bf16[192,1280]{1,0:T(8,128)(2,1)S(1)}, bf16[192,1280]{1,0:T(8,128)(2,1)}, u32[]{:S(2)}) copy-start(bf16[192,1280]{1,0:T(8,128)(2,1)} %copy-done.4) | copy-start | bytes 1474564
  161.4 3.5 %copy-start.8 = (f32[2,192,8]{2,1,0:T(8,128)S(1)}, f32[2,192,8]{2,1,0:T(8,128)}, u32[]{:S(2)}) copy-start(f32[2,192,8]{2,1,0:T(8,128)} %copy-done.7) | copy-start | bytes 36868
  164.9 1.0 copy-start.6
  183.7 31.0 %copy-start.10 = (f32[2,192,1280]{2,1,0:T(8,128)S(1)}, f32[2,192,1280]{2,1,0:T(8,128)}, u32[]{:S(2)}) copy-start(f32[2,192,1280]{2,1,0:T(8,128)} %get-tuple-element.46) | copy-start | bytes 5898244
  183.7 26.6 %collective-permute-start.6 = (bf16[2,192,1280]{2,1,0:T(8,128)(2,1)}, bf16[2,192,1280]{2,1,0:T(8,128)(2,1)}, u32[]{:S(2)}, u32[]{:S(2)}) collective-permute-start(bf16[2,192,1280]{2,1,0:T(8,128)(2,1)} %get-tuple-element.47), channel_id=1, source_target_pairs={{0,8},{8,16},{16,24},{24,32},{32,40},{40,48},{48,56},{56,64},{64,7... | collective-permute-start | bytes 2949128 | tf_op jit(solution)/shard_map/ppermute | solution.py:20
  186.9 27.8 %collective-permute-start.7 = (bf16[2,192,1280]{2,1,0:T(8,128)(2,1)}, bf16[2,192,1280]{2,1,0:T(8,128)(2,1)}, u32[]{:S(2)}, u32[]{:S(2)}) collective-permute-start(bf16[2,192,1280]{2,1,0:T(8,128)(2,1)} %get-tuple-element.48), channel_id=1, source_target_pairs={{8,0},{16,8},{24,16},{32,24},{40,32},{48,40},{56,48},{64,56},{72,6... | collective-permute-start | bytes 2949128 | tf_op jit(solution)/shard_map/ppermute | solution.py:20
  194.9 40.5 %all-to-all-start.2 = ((bf16[32,8,1280]{2,1,0:T(8,128)(2,1)}), bf16[32,8,1280]{2,1,0:T(8,128)(2,1)S(1)}, u32[]{:S(2)}, u32[]{:S(2)}) async-start(bf16[32,8,1280]{2,1,0:T(8,128)(2,1)} %pad_maximum_fusion.1), calls=%async_computation.4 | async-start | bytes 1310720 | tf_op jit(solution)/shard_map/all_to_all | solution.py:319
Sparse Core Ops, SparseCore 0:
  9.9 46.5 all-gather.7
  58.9 31.0 all-gather.5
  119.7 32.9 reduce-scatter.2
  165.0 27.3 reduce-scatter.4
